TPU v7x, 32 devices: a whole 2x2x4 slice. The times are simulated.
32 devices in a mesh: fsdp: 8 (over z, y), tensor: 4 (over x, core).
Axes of the slice: x: 2, y: 2, z: 4, core: 2. Of those that a mesh axis runs over, the one named last changes fastest.
Arguments:
- inputs: bfloat16 [4096, 2048], P(('fsdp', 'tensor')), may hold values from -6 to 6
- seg_ids: int32 [4096], P('fsdp'), may hold values from 0 to 4095, as said below
- positions: int32 [4096], P('fsdp'), may hold values from 0 to 766, as said below
- w_query: bfloat16 [2048, 2048], P('fsdp', 'tensor'), may hold values from -0.125 to 0.125
- w_key: bfloat16 [2048, 2048], P('fsdp', 'tensor'), may hold values from -0.125 to 0.125
- w_value: bfloat16 [2048, 2048], P('fsdp', 'tensor'), may hold values from -0.125 to 0.125
- w_out: bfloat16 [2048, 2048], P('tensor', 'fsdp'), may hold values from -0.125 to 0.125
- query_gain: bfloat16 [16, 128], P('tensor', 'fsdp'), may hold values from 0.5 to 1.5
- key_gain: bfloat16 [16, 128], P('tensor', 'fsdp'), may hold values from 0.5 to 1.5
- attn_gain: bfloat16 [2048], P('fsdp'), may hold values from 0.5 to 1.5
- w_gate: bfloat16 [2048, 8192], P('fsdp', 'tensor'), may hold values from -0.125 to 0.125
- w_up: bfloat16 [2048, 8192], P('fsdp', 'tensor'), may hold values from -0.125 to 0.125
- w_down: bfloat16 [8192, 2048], P('tensor', 'fsdp'), may hold values from -0.0625 to 0.0625
- ffn_gain: bfloat16 [2048], P('fsdp'), may hold values from 0.5 to 1.5
- out_grad: bfloat16 [4096, 2048], P(('fsdp', 'tensor')), may hold values from -6 to 6
Outputs:
- output: bfloat16 [4096, 2048], P(('fsdp', 'tensor'))
- grad_inputs: float32 [4096, 2048], P(('fsdp', 'tensor'))
- grad_query: float32 [2048, 2048], P('fsdp', 'tensor')
- grad_key: float32 [2048, 2048], P('fsdp', 'tensor')
- grad_value: float32 [2048, 2048], P('fsdp', 'tensor')
- grad_out: float32 [2048, 2048], P('tensor', 'fsdp')
- grad_query_gain: float32 [16, 128], P('tensor', 'fsdp')
- grad_key_gain: float32 [16, 128], P('tensor', 'fsdp')
- grad_attn_gain: float32 [2048], P('fsdp')
- grad_gate: float32 [2048, 8192], P('fsdp', 'tensor')
- grad_up: float32 [2048, 8192], P('fsdp', 'tensor')
- grad_down: float32 [8192, 2048], P('tensor', 'fsdp')
- grad_ffn_gain: float32 [2048], P('fsdp')
Inputs may be any that keep to these rules, and one draw needn't show every extreme that they name: seg_ids holds, for each token, the index of the first token of its sequence; no sequence crosses a block of 512 tokens of one fsdp index; each block holds one sequence longer than three quarters of it; in some block one sequence fills it; the last token of all is a sequence of its own. positions count up by one within each sequence from an offset of at most 255.
All inputs are finite; a program needn't handle non-finite values.
Results may differ from a plain program's by a relative error of at most 0.02.
Values may be sent and summed in bfloat16 or wider, within the bound.
A program may use at most 192 MiB of HBM per device.

v0:
```python
import jax
import jax.numpy as jnp
from jax import lax
from jax.sharding import PartitionSpec as P

HD = 128


NORM_EPS = 1e-06
ROPE_THETA = 500000.0


def rope_tables(positions, head_size):
    half_size = head_size // 2
    freq = ROPE_THETA ** (-(jnp.arange(half_size, dtype=jnp.float32) * 2.0) / head_size)
    angle = positions.astype(jnp.float32)[:, None] * freq[None, :]
    return (jnp.cos(angle), jnp.sin(angle))


def rotate(values, cosine, sine):
    half_size = values.shape[-1] // 2
    first = values[..., :half_size]
    second = values[..., half_size:]
    cosine = cosine[:, None, :]
    sine = sine[:, None, :]
    return jnp.concatenate(
        [first * cosine - second * sine, second * cosine + first * sine], axis=-1
    )


def normalize(values):
    inverse = lax.rsqrt(jnp.mean(values * values, axis=1, keepdims=True) + NORM_EPS)
    return (values * inverse, inverse)


def norm_back(grad_scaled, normed, inverse):
    return inverse * (grad_scaled - normed * jnp.mean(grad_scaled * normed, axis=1, keepdims=True))


def contract_last(left, right):
    return lax.dot_general(
        left, right, (((1,), (1,)), ((), ())), preferred_element_type=jnp.float32
    )


def contract_first(left, right):
    return lax.dot_general(
        left, right, (((0,), (0,)), ((), ())), preferred_element_type=jnp.float32
    )


def block_mask(seg_ids, row_start, block_rows):
    query_index = row_start + jnp.arange(block_rows, dtype=jnp.int32)
    key_index = jnp.arange(seg_ids.shape[0], dtype=jnp.int32)
    return (seg_ids[:, None] == seg_ids[None, :]) & (key_index[None, :] <= query_index[:, None])


def attend_forward(queries, key_rows, values, seg_ids, block_rows):
    row_count = queries.shape[0]
    score_scale = queries.shape[-1] ** (-0.5)

    def one_block(block_index):
        row_start = block_index * block_rows
        scores = (
            jnp.einsum("qhd,khd->hqk", queries, key_rows, preferred_element_type=jnp.float32)
            * score_scale
        )
        scores = jnp.where(block_mask(seg_ids, row_start, block_rows)[None], scores, -1e30)
        row_max = jnp.max(scores, axis=-1, keepdims=True)
        exp_scores = jnp.exp(scores - row_max)
        row_total = jnp.sum(exp_scores, axis=-1, keepdims=True)
        weights_low = (exp_scores / row_total).astype(jnp.bfloat16)
        mixed_out = jnp.einsum(
            "hqk,khd->qhd", weights_low, values, preferred_element_type=jnp.float32
        )
        return (mixed_out, (row_max + jnp.log(row_total))[..., 0])

    mixed_out, log_total = lax.map(one_block, jnp.arange(row_count // block_rows, dtype=jnp.int32))
    return (mixed_out.reshape(row_count, -1), log_total)


def attend_backward(queries, key_rows, values, grad_mixed, log_total, seg_ids, block_rows):
    row_count = queries.shape[0]
    score_scale = queries.shape[-1] ** (-0.5)

    def one_block(carry, block_index):
        grad_keys, grad_values = carry
        row_start = block_index * block_rows
        scores = (
            jnp.einsum("qhd,khd->hqk", queries, key_rows, preferred_element_type=jnp.float32)
            * score_scale
        )
        allowed = block_mask(seg_ids, row_start, block_rows)[None]
        probs = jnp.where(allowed, jnp.exp(scores - log_total[block_index][..., None]), 0.0)
        grad_probs = jnp.einsum(
            "qhd,khd->hqk", grad_mixed, values, preferred_element_type=jnp.float32
        )
        inner = jnp.sum(probs * grad_probs, axis=-1, keepdims=True)
        grad_scores = (probs * (grad_probs - inner)).astype(jnp.bfloat16)
        grad_query = (
            jnp.einsum("hqk,khd->qhd", grad_scores, key_rows, preferred_element_type=jnp.float32)
            * score_scale
        )
        grad_keys = (
            grad_keys
            + jnp.einsum("hqk,qhd->khd", grad_scores, queries, preferred_element_type=jnp.float32)
            * score_scale
        )
        grad_values = grad_values + jnp.einsum(
            "hqk,qhd->khd",
            probs.astype(jnp.bfloat16),
            grad_mixed,
            preferred_element_type=jnp.float32,
        )
        return ((grad_keys, grad_values), grad_query)

    zero_rows = jnp.zeros(key_rows.shape, jnp.float32)
    (grad_keys, grad_values), grad_query = lax.scan(
        one_block, (zero_rows, zero_rows), jnp.arange(row_count // block_rows, dtype=jnp.int32)
    )
    return (grad_query.reshape(key_rows.shape), grad_keys, grad_values)


def local(
    inputs,
    seg_ids,
    positions,
    w_query,
    w_key,
    w_value,
    w_out,
    query_gain,
    key_gain,
    attn_gain,
    w_gate,
    w_up,
    w_down,
    ffn_gain,
    out_grad,
):
    gathered = (
        lax.all_gather(w_query, "fsdp", axis=0, tiled=True),
        lax.all_gather(w_key, "fsdp", axis=0, tiled=True),
        lax.all_gather(w_value, "fsdp", axis=0, tiled=True),
        lax.all_gather(w_out, "fsdp", axis=1, tiled=True),
        lax.all_gather(query_gain, "fsdp", axis=1, tiled=True),
        lax.all_gather(key_gain, "fsdp", axis=1, tiled=True),
        lax.all_gather(attn_gain, "fsdp", axis=0, tiled=True),
        lax.all_gather(w_gate, "fsdp", axis=0, tiled=True),
        lax.all_gather(w_up, "fsdp", axis=0, tiled=True),
        lax.all_gather(w_down, "fsdp", axis=1, tiled=True),
        lax.all_gather(ffn_gain, "fsdp", axis=0, tiled=True),
    )
    (
        full_query,
        full_key,
        full_value,
        full_out,
        gain_query,
        gain_key,
        gain_attn,
        full_gate,
        full_up,
        full_down,
        gain_ffn,
    ) = gathered
    heads_local = gain_query.shape[0]
    gain_query = gain_query.reshape(-1).astype(jnp.float32)
    gain_key = gain_key.reshape(-1).astype(jnp.float32)
    gain_attn = gain_attn.astype(jnp.float32)
    gain_ffn = gain_ffn.astype(jnp.float32)
    width = inputs.shape[1]
    group_rows = seg_ids.shape[0]
    block_rows = min(512, group_rows)
    rows_in = lax.all_gather(inputs, "tensor", axis=0, tiled=True)
    query_raw = jnp.dot(rows_in, full_query, preferred_element_type=jnp.float32)
    key_raw = jnp.dot(rows_in, full_key, preferred_element_type=jnp.float32)
    value_raw = jnp.dot(rows_in, full_value, preferred_element_type=jnp.float32)
    query_sq, key_sq = lax.psum(
        (jnp.sum(query_raw * query_raw, axis=1), jnp.sum(key_raw * key_raw, axis=1)), "tensor"
    )
    query_inv = lax.rsqrt(query_sq / width + NORM_EPS)[:, None]
    key_inv = lax.rsqrt(key_sq / width + NORM_EPS)[:, None]
    query_hat = query_raw * query_inv
    key_hat = key_raw * key_inv
    cosine, sine = rope_tables(positions, HD)
    query_rot = rotate(
        (query_hat * gain_query).reshape(group_rows, heads_local, HD), cosine, sine
    ).astype(jnp.bfloat16)
    key_rot = rotate(
        (key_hat * gain_key).reshape(group_rows, heads_local, HD), cosine, sine
    ).astype(jnp.bfloat16)
    value_low = value_raw.astype(jnp.bfloat16).reshape(group_rows, heads_local, HD)
    mixed_heads, log_total = attend_forward(query_rot, key_rot, value_low, seg_ids, block_rows)
    mixed_low = mixed_heads.astype(jnp.bfloat16)
    attn_raw = lax.psum_scatter(
        jnp.dot(mixed_low, full_out, preferred_element_type=jnp.float32),
        "tensor",
        scatter_dimension=0,
        tiled=True,
    )
    attn_normed, attn_inv = normalize(attn_raw)
    resid = inputs.astype(jnp.float32) + attn_normed * gain_attn
    rows_mid = lax.all_gather(resid.astype(jnp.bfloat16), "tensor", axis=0, tiled=True)
    gate_raw = jnp.dot(rows_mid, full_gate, preferred_element_type=jnp.float32)
    up_raw = jnp.dot(rows_mid, full_up, preferred_element_type=jnp.float32)
    hidden_low = (jax.nn.silu(gate_raw) * up_raw).astype(jnp.bfloat16)
    ffn_raw = lax.psum_scatter(
        jnp.dot(hidden_low, full_down, preferred_element_type=jnp.float32),
        "tensor",
        scatter_dimension=0,
        tiled=True,
    )
    ffn_normed, ffn_inv = normalize(ffn_raw)
    output = (resid + ffn_normed * gain_ffn).astype(jnp.bfloat16)
    grad_top = out_grad.astype(jnp.float32)
    partial_ffn_gain = jnp.sum(grad_top * ffn_normed, axis=0)
    grad_ffn = norm_back(grad_top * gain_ffn, ffn_normed, ffn_inv).astype(jnp.bfloat16)
    rows_grad_ffn = lax.all_gather(grad_ffn, "tensor", axis=0, tiled=True)
    grad_hidden = contract_last(rows_grad_ffn, full_down)
    wgrad_down = contract_first(hidden_low, rows_grad_ffn)
    gate_sig = jax.nn.sigmoid(gate_raw)
    grad_gate_act = (grad_hidden * up_raw * gate_sig * (1.0 + gate_raw * (1.0 - gate_sig))).astype(
        jnp.bfloat16
    )
    grad_up_act = (grad_hidden * (gate_raw * gate_sig)).astype(jnp.bfloat16)
    wgrad_gate = contract_first(rows_mid, grad_gate_act)
    wgrad_up = contract_first(rows_mid, grad_up_act)
    grad_mid = lax.psum_scatter(
        contract_last(grad_gate_act, full_gate) + contract_last(grad_up_act, full_up),
        "tensor",
        scatter_dimension=0,
        tiled=True,
    )
    grad_resid = grad_top + grad_mid
    partial_attn_gain = jnp.sum(grad_resid * attn_normed, axis=0)
    grad_attn = norm_back(grad_resid * gain_attn, attn_normed, attn_inv).astype(jnp.bfloat16)
    rows_grad_attn = lax.all_gather(grad_attn, "tensor", axis=0, tiled=True)
    grad_mixed = (
        contract_last(rows_grad_attn, full_out)
        .astype(jnp.bfloat16)
        .reshape(group_rows, heads_local, HD)
    )
    wgrad_out = contract_first(mixed_low, rows_grad_attn)
    grad_qrot, grad_krot, grad_vlow = attend_backward(
        query_rot, key_rot, value_low, grad_mixed, log_total, seg_ids, block_rows
    )
    grad_qnorm = rotate(grad_qrot, cosine, -sine).reshape(group_rows, -1)
    grad_knorm = rotate(grad_krot, cosine, -sine).reshape(group_rows, -1)
    grad_qhat = grad_qnorm * gain_query
    grad_khat = grad_knorm * gain_key
    inner_query, inner_key, gain_sums = lax.psum(
        (
            jnp.sum(grad_qhat * query_hat, axis=1),
            jnp.sum(grad_khat * key_hat, axis=1),
            jnp.stack([partial_attn_gain, partial_ffn_gain]),
        ),
        "tensor",
    )
    grad_query_raw = (query_inv * (grad_qhat - query_hat * (inner_query / width)[:, None])).astype(
        jnp.bfloat16
    )
    grad_key_raw = (key_inv * (grad_khat - key_hat * (inner_key / width)[:, None])).astype(
        jnp.bfloat16
    )
    grad_value_raw = grad_vlow.reshape(group_rows, -1).astype(jnp.bfloat16)
    wgrad_qgain = jnp.sum(grad_qnorm * query_hat, axis=0).reshape(heads_local, HD)
    wgrad_kgain = jnp.sum(grad_knorm * key_hat, axis=0).reshape(heads_local, HD)
    grad_rows = lax.psum_scatter(
        (
            contract_last(grad_query_raw, full_query)
            + contract_last(grad_key_raw, full_key)
            + contract_last(grad_value_raw, full_value)
        ).astype(jnp.bfloat16),
        "tensor",
        scatter_dimension=0,
        tiled=True,
    ).astype(jnp.float32)
    grad_inputs = grad_resid + grad_rows
    wgrad_query = contract_first(rows_in, grad_query_raw)
    wgrad_key = contract_first(rows_in, grad_key_raw)
    wgrad_value = contract_first(rows_in, grad_value_raw)
    all_sums = (
        lax.psum_scatter(
            wgrad_query.astype(jnp.bfloat16), "fsdp", scatter_dimension=0, tiled=True
        ).astype(jnp.float32),
        lax.psum_scatter(
            wgrad_key.astype(jnp.bfloat16), "fsdp", scatter_dimension=0, tiled=True
        ).astype(jnp.float32),
        lax.psum_scatter(
            wgrad_value.astype(jnp.bfloat16), "fsdp", scatter_dimension=0, tiled=True
        ).astype(jnp.float32),
        lax.psum_scatter(
            wgrad_out.astype(jnp.bfloat16), "fsdp", scatter_dimension=1, tiled=True
        ).astype(jnp.float32),
        lax.psum_scatter(
            wgrad_qgain.astype(jnp.bfloat16), "fsdp", scatter_dimension=1, tiled=True
        ).astype(jnp.float32),
        lax.psum_scatter(
            wgrad_kgain.astype(jnp.bfloat16), "fsdp", scatter_dimension=1, tiled=True
        ).astype(jnp.float32),
        lax.psum_scatter(
            gain_sums.astype(jnp.bfloat16), "fsdp", scatter_dimension=1, tiled=True
        ).astype(jnp.float32),
        lax.psum_scatter(
            wgrad_gate.astype(jnp.bfloat16), "fsdp", scatter_dimension=0, tiled=True
        ).astype(jnp.float32),
        lax.psum_scatter(
            wgrad_up.astype(jnp.bfloat16), "fsdp", scatter_dimension=0, tiled=True
        ).astype(jnp.float32),
        lax.psum_scatter(
            wgrad_down.astype(jnp.bfloat16), "fsdp", scatter_dimension=1, tiled=True
        ).astype(jnp.float32),
    )
    (
        sum_query,
        sum_key,
        sum_value,
        sum_out,
        sum_qgain,
        sum_kgain,
        sum_gains,
        sum_gate,
        sum_up,
        sum_down,
    ) = all_sums
    return (
        output,
        grad_inputs,
        sum_query,
        sum_key,
        sum_value,
        sum_out,
        sum_qgain,
        sum_kgain,
        sum_gains[0],
        sum_gate,
        sum_up,
        sum_down,
        sum_gains[1],
    )


def solution(mesh):
    placed = (
        P(("fsdp", "tensor"), None),
        P("fsdp"),
        P("fsdp"),
        P("fsdp", "tensor"),
        P("fsdp", "tensor"),
        P("fsdp", "tensor"),
        P("tensor", "fsdp"),
        P("tensor", "fsdp"),
        P("tensor", "fsdp"),
        P("fsdp"),
        P("fsdp", "tensor"),
        P("fsdp", "tensor"),
        P("tensor", "fsdp"),
        P("fsdp"),
        P(("fsdp", "tensor"), None),
    )
    return jax.shard_map(
        local,
        mesh=mesh,
        in_specs=placed,
        out_specs=(
            P(("fsdp", "tensor"), None),
            P(("fsdp", "tensor"), None),
            P("fsdp", "tensor"),
            P("fsdp", "tensor"),
            P("fsdp", "tensor"),
            P("tensor", "fsdp"),
            P("tensor", "fsdp"),
            P("tensor", "fsdp"),
            P("fsdp"),
            P("fsdp", "tensor"),
            P("fsdp", "tensor"),
            P("tensor", "fsdp"),
            P("fsdp"),
        ),
        check_vma=False,
    )
```

profile of v0, /device:TPU:0, one launch (start us, length us, event | category | flops | bytes accessed | tf_op | source)
XLA Modules:
  0.0 1848.8 jit_solution(7418325141897786769)
XLA Ops:
  11.3 22.5 %all-gather = bf16[8,16,4]{1,2,0:T(4,128)(2,1)S(1)} all-gather(bf16[1,16,4]{1,2,0:T(4,128)(2,1)} %bitcast.152), channel_id=1, replica_groups=mesh['fsdp'=8,'tensor'=4] {'fsdp'}, dimensions={0}, use_global_device_ids=true | all-gather | bytes 1152 | tf_op jit(solution)/shard_map/all_gather | solution.py:146
  33.9 16.7 all-gather.1
  53.4 32.9 %all-gather.20.cloned.1.call-done = bf16[2048,512]{1,0:T(8,128)(2,1)} async-done(((bf16[256,512]{1,0:T(8,128)(2,1)}), bf16[2048,512]{1,0:T(8,128)(2,1)}) %all-gather.20.cloned.1.call-update) | async-done | bytes 2097168 | tf_op jit(solution)/shard_map/all_gather | solution.py:142
  89.9 46.4 %all-gather.22.cloned.1.call-done = bf16[2048,512]{1,0:T(8,128)(2,1)} async-done(((bf16[256,512]{1,0:T(8,128)(2,1)}), bf16[2048,512]{1,0:T(8,128)(2,1)}) %all-gather.22.cloned.1.call-update) | async-done | bytes 2097168 | tf_op jit(solution)/shard_map/all_gather | solution.py:143
  161.2 24.9 %all-gather.18.cloned.1.call-done = bf16[2048,512]{1,0:T(8,128)(2,1)} async-done(((bf16[256,512]{1,0:T(8,128)(2,1)}), bf16[2048,512]{1,0:T(8,128)(2,1)}) %all-gather.18.cloned.1.call-update) | async-done | bytes 2097168 | tf_op jit(solution)/shard_map/all_gather | solution.py:144
  191.4 46.1 %all-gather.24.cloned.1.call-done = bf16[512,2048]{1,0:T(8,128)(2,1)} async-done(((bf16[512,256]{1,0:T(8,128)(2,1)}), bf16[512,2048]{1,0:T(8,128)(2,1)}) %all-gather.24.cloned.1.call-update) | async-done | bytes 2097168 | tf_op jit(solution)/shard_map/all_gather | solution.py:145
  243.3 17.9 all-gather.2
  261.2 24.1 %reduce-scatter.21.cloned.1.call-done = f32[128,2048]{1,0:T(8,128)} async-done(((f32[512,2048]{1,0:T(8,128)}), f32[128,2048]{1,0:T(8,128)}) %reduce-scatter.21.cloned.1.call-update) | async-done | bytes 1048592 | tf_op jit(solution)/shard_map/reduce_scatter | solution.py:196
  290.4 122.3 %all-gather.28.cloned.1.call-done = bf16[2048,2048]{1,0:T(8,128)(2,1)} async-done(((bf16[256,2048]{1,0:T(8,128)(2,1)}), bf16[2048,2048]{1,0:T(8,128)(2,1)}) %all-gather.28.cloned.1.call-update) | async-done | bytes 8388624 | tf_op jit(solution)/shard_map/all_gather | solution.py:149
  412.6 23.0 %all-gather.26.cloned.1.call-done = bf16[512,2048]{1,0:T(8,128)(2,1)} async-done(((bf16[128,2048]{1,0:T(8,128)(2,1)}), bf16[512,2048]{1,0:T(8,128)(2,1)}) %all-gather.26.cloned.1.call-update) | async-done | bytes 2097168 | tf_op jit(solution)/shard_map/all_gather | solution.py:204
  435.6 10.6 fusion.42
  446.3 116.7 %all-gather.30.cloned.1.call-done = bf16[2048,2048]{1,0:T(8,128)(2,1)} async-done(((bf16[256,2048]{1,0:T(8,128)(2,1)}), bf16[2048,2048]{1,0:T(8,128)(2,1)}) %all-gather.30.cloned.1.call-update) | async-done | bytes 8388624 | tf_op jit(solution)/shard_map/all_gather | solution.py:150
  563.0 10.8 multiply_convert_fusion.3
  573.8 114.9 %all-gather.32.cloned.1.call-done = bf16[2048,2048]{1,0:T(8,128)(2,1)} async-done(((bf16[2048,256]{1,0:T(8,128)(2,1)}), bf16[2048,2048]{1,0:T(8,128)(2,1)}) %all-gather.32.cloned.1.call-update) | async-done | bytes 8388624 | tf_op jit(solution)/shard_map/all_gather | solution.py:151
  688.7 10.5 fusion.43
  699.8 17.7 all-gather.3
  717.6 24.5 %reduce-scatter.23.cloned.1.call-done = f32[128,2048]{1,0:T(8,128)} async-done(((f32[512,2048]{1,0:T(8,128)}), f32[128,2048]{1,0:T(8,128)}) %reduce-scatter.23.cloned.1.call-update) | async-done | bytes 1048592 | tf_op jit(solution)/shard_map/reduce_scatter | solution.py:208
  747.9 22.3 %all-gather.34.cloned.1.call-done = bf16[512,2048]{1,0:T(8,128)(2,1)} async-done(((bf16[128,2048]{1,0:T(8,128)(2,1)}), bf16[512,2048]{1,0:T(8,128)(2,1)}) %all-gather.34.cloned.1.call-update) | async-done | bytes 2097168 | tf_op jit(solution)/shard_map/all_gather | solution.py:219
  770.1 11.9 multiply_convert_fusion.1
  800.2 44.6 %reduce-scatter.25.cloned.1.call-done = f32[128,2048]{1,0:T(8,128)} async-done(((f32[512,2048]{1,0:T(8,128)}), f32[128,2048]{1,0:T(8,128)}) %reduce-scatter.25.cloned.1.call-update) | async-done | bytes 1048592 | tf_op jit(solution)/shard_map/reduce_scatter | solution.py:229
  849.4 22.5 %all-gather.36.cloned.1.call-done = bf16[512,2048]{1,0:T(8,128)(2,1)} async-done(((bf16[128,2048]{1,0:T(8,128)(2,1)}), bf16[512,2048]{1,0:T(8,128)(2,1)}) %all-gather.36.cloned.1.call-update) | async-done | bytes 2097168 | tf_op jit(solution)/shard_map/all_gather | solution.py:238
  896.9 10.4 all-reduce
  968.2 31.0 %reduce-scatter.43.cloned.1.call-done = bf16[16,4]{1,0:T(8,128)(2,1)} async-done(((bf16[128,4]{1,0:T(8,128)(2,1)}), bf16[16,4]{1,0:T(8,128)(2,1)}) %reduce-scatter.43.cloned.1.call-update) | async-done | bytes 144
  1000.5 63.8 %reduce-scatter.47.cloned.1.call-done = bf16[256,2]{1,0:T(8,128)(2,1)} async-done(((bf16[2048,2]{1,0:T(8,128)(2,1)}), bf16[256,2]{1,0:T(8,128)(2,1)}) %reduce-scatter.47.cloned.1.call-update) | async-done | bytes 1040
  1065.8 69.3 %reduce-scatter.35.cloned.1.call-done = bf16[512,256]{1,0:T(8,128)(2,1)} async-done(((bf16[512,2048]{1,0:T(8,128)(2,1)}), bf16[512,256]{1,0:T(8,128)(2,1)}) %reduce-scatter.35.cloned.1.call-update) | async-done | bytes 262160 | tf_op jit(solution)/shard_map/reduce_scatter | solution.py:293
  1136.9 69.2 %reduce-scatter.33.cloned.1.call-done = bf16[256,512]{0,1:T(8,128)(2,1)} async-done(((bf16[2048,512]{0,1:T(8,128)(2,1)}), bf16[256,512]{0,1:T(8,128)(2,1)}) %reduce-scatter.33.cloned.1.call-update) | async-done | bytes 262160 | tf_op jit(solution)/shard_map/reduce_scatter | solution.py:290
  1208.0 68.8 %reduce-scatter.31.cloned.1.call-done = bf16[256,512]{0,1:T(8,128)(2,1)} async-done(((bf16[2048,512]{0,1:T(8,128)(2,1)}), bf16[256,512]{0,1:T(8,128)(2,1)}) %reduce-scatter.31.cloned.1.call-update) | async-done | bytes 262160 | tf_op jit(solution)/shard_map/reduce_scatter | solution.py:287
  1278.7 69.6 %reduce-scatter.29.cloned.1.call-done = bf16[256,512]{0,1:T(8,128)(2,1)} async-done(((bf16[2048,512]{0,1:T(8,128)(2,1)}), bf16[256,512]{0,1:T(8,128)(2,1)}) %reduce-scatter.29.cloned.1.call-update) | async-done | bytes 262160 | tf_op jit(solution)/shard_map/reduce_scatter | solution.py:284
  1350.2 31.7 %reduce-scatter.27.cloned.1.call-done = bf16[128,2048]{1,0:T(8,128)(2,1)} async-done(((bf16[512,2048]{1,0:T(8,128)(2,1)}), bf16[128,2048]{1,0:T(8,128)(2,1)}) %reduce-scatter.27.cloned.1.call-update) | async-done | bytes 524304 | tf_op jit(solution)/shard_map/reduce_scatter | solution.py:269
  1384.1 151.3 %reduce-scatter.41.cloned.1.call-done = bf16[2048,256]{1,0:T(8,128)(2,1)} async-done(((bf16[2048,2048]{1,0:T(8,128)(2,1)}), bf16[2048,256]{1,0:T(8,128)(2,1)}) %reduce-scatter.41.cloned.1.call-update) | async-done | bytes 1048592 | tf_op jit(solution)/shard_map/reduce_scatter | solution.py:311
  1538.1 148.9 %reduce-scatter.39.cloned.1.call-done = bf16[256,2048]{1,0:T(8,128)(2,1)} async-done(((bf16[2048,2048]{1,0:T(8,128)(2,1)}), bf16[256,2048]{1,0:T(8,128)(2,1)}) %reduce-scatter.39.cloned.1.call-update) | async-done | bytes 1048592 | tf_op jit(solution)/shard_map/reduce_scatter | solution.py:308
  1689.8 149.3 %reduce-scatter.37.cloned.1.call-done = bf16[256,2048]{1,0:T(8,128)(2,1)} async-done(((bf16[2048,2048]{1,0:T(8,128)(2,1)}), bf16[256,2048]{1,0:T(8,128)(2,1)}) %reduce-scatter.37.cloned.1.call-update) | async-done | bytes 1048592 | tf_op jit(solution)/shard_map/reduce_scatter | solution.py:305
  (225 shorter events, 186.6 us)
Async XLA Ops:
  7.2 46.2 %all-gather.16.cloned.1.call-start = ((), (), s32[]{:S(2)}) async-start(), calls=%async_computation.14 | async-start | bytes 2621440 | tf_op jit(solution)/shard_map/all_gather | solution.py:175
  7.9 78.4 %all-gather.20.cloned.1.call-start = ((), (), s32[]{:S(2)}) async-start(), calls=%async_computation.16 | async-start | bytes 2359296 | tf_op jit(solution)/shard_map/all_gather | solution.py:142
  8.7 127.6 %all-gather.22.cloned.1.call-start = ((), (), s32[]{:S(2)}) async-start(), calls=%async_computation.17 | async-start | bytes 2359296 | tf_op jit(solution)/shard_map/all_gather | solution.py:143
  9.4 176.7 %all-gather.18.cloned.1.call-start = ((), (), s32[]{:S(2)}) async-start(), calls=%async_computation.15 | async-start | bytes 2359296 | tf_op jit(solution)/shard_map/all_gather | solution.py:144
  10.0 227.6 %all-gather.24.cloned.1.call-start = ((), (), s32[]{:S(2)}) async-start(), calls=%async_computation.18 | async-start | bytes 2359296 | tf_op jit(solution)/shard_map/all_gather | solution.py:145
  10.6 274.8 %reduce-scatter.21.cloned.1.call-start = ((), (), s32[]{:S(2)}) async-start(), calls=%async_computation.19 | async-start | bytes 5242880 | tf_op jit(solution)/shard_map/reduce_scatter | solution.py:196
  53.4 100.6 %copy-start.23 = (f32[512,64]{1,0:T(8,128)}, f32[512,64]{1,0:T(8,128)S(1)}, u32[]{:S(2)}) copy-start(f32[512,64]{1,0:T(8,128)S(1)} %get-tuple-element.151) | copy-start | bytes 393220
  89.9 60.3 %copy-start.7 = (f32[512,512]{0,1:T(8,128)}, f32[512,512]{0,1:T(8,128)S(1)}, u32[]{:S(2)}) copy-start(f32[512,512]{0,1:T(8,128)S(1)} %get-tuple-element.157) | copy-start | bytes 3145732
  191.4 51.1 %copy-start.33 = (bf16[4,128,512]{2,1,0:T(8,128)(2,1)}, bf16[4,128,512]{2,1,0:T(8,128)(2,1)S(1)}, u32[]{:S(2)}) copy-start(bf16[4,128,512]{2,1,0:T(8,128)(2,1)S(1)} %fusion.15) | copy-start | bytes 1572868
  242.5 170.2 %all-gather.28.cloned.1.call-start = ((), (), s32[]{:S(2)}) async-start(), calls=%async_computation.21 | async-start | bytes 9437184 | tf_op jit(solution)/shard_map/all_gather | solution.py:149
  243.2 192.4 %all-gather.26.cloned.1.call-start = ((), (), s32[]{:S(2)}) async-start(), calls=%async_computation.20 | async-start | bytes 2621440 | tf_op jit(solution)/shard_map/all_gather | solution.py:204
  289.0 274.0 %all-gather.30.cloned.1.call-start = ((), (), s32[]{:S(2)}) async-start(), calls=%async_computation.22 | async-start | bytes 9437184 | tf_op jit(solution)/shard_map/all_gather | solution.py:150
  289.7 398.9 %all-gather.32.cloned.1.call-start = ((), (), s32[]{:S(2)}) async-start(), calls=%async_computation.23 | async-start | bytes 9437184 | tf_op jit(solution)/shard_map/all_gather | solution.py:151
  290.3 451.8 %reduce-scatter.23.cloned.1.call-start = ((), (), s32[]{:S(2)}) async-start(), calls=%async_computation.24 | async-start | bytes 5242880 | tf_op jit(solution)/shard_map/reduce_scatter | solution.py:208
  435.6 127.3 %copy-start.36 = (bf16[512,2048]{1,0:T(8,128)(2,1)S(1)}, bf16[512,2048]{1,0:T(8,128)(2,1)}, u32[]{:S(2)}) copy-start(bf16[512,2048]{1,0:T(8,128)(2,1)} %all-gather.26.cloned.1.call-done) | copy-start | bytes 6291460
  699.2 70.9 %all-gather.34.cloned.1.call-start = ((), (), s32[]{:S(2)}) async-start(), calls=%async_computation.25 | async-start | bytes 2621440 | tf_op jit(solution)/shard_map/all_gather | solution.py:219
  747.4 97.4 %reduce-scatter.25.cloned.1.call-start = ((), (), s32[]{:S(2)}) async-start(), calls=%async_computation.26 | async-start | bytes 5242880 | tf_op jit(solution)/shard_map/reduce_scatter | solution.py:229
  800.1 44.7 %copy-start.3 = (f32[128,2048]{1,0:T(8,128)S(1)}, f32[128,2048]{1,0:T(8,128)}, u32[]{:S(2)}) copy-start(f32[128,2048]{1,0:T(8,128)} %reduce-scatter.21.cloned.1.call-done) | copy-start | bytes 3145732
  800.1 46.3 %copy-start.4 = (f32[128,2048]{1,0:T(8,128)S(1)}, f32[128,2048]{1,0:T(8,128)}, u32[]{:S(2)}) copy-start(f32[128,2048]{1,0:T(8,128)} %reduce-scatter.23.cloned.1.call-done) | copy-start | bytes 3145732
  800.2 71.8 %all-gather.36.cloned.1.call-start = ((), (), s32[]{:S(2)}) async-start(), calls=%async_computation.27 | async-start | bytes 2621440 | tf_op jit(solution)/shard_map/all_gather | solution.py:238
  849.2 117.6 %reduce-scatter.45.cloned.1.call-start = ((), (), s32[]{:S(2)}) async-start(), calls=%async_computation.37 | async-start | bytes 36864
  889.1 110.1 %reduce-scatter.43.cloned.1.call-start = ((), (), s32[]{:S(2)}) async-start(), calls=%async_computation.36 | async-start | bytes 36864
  896.8 167.5 %reduce-scatter.47.cloned.1.call-start = ((), (), s32[]{:S(2)}) async-start(), calls=%async_computation.38 | async-start | bytes 589824
  908.3 226.8 %reduce-scatter.35.cloned.1.call-start = ((), (), s32[]{:S(2)}) async-start(), calls=%async_computation.32 | async-start | bytes 2359296 | tf_op jit(solution)/shard_map/reduce_scatter | solution.py:293
  912.8 293.3 %reduce-scatter.33.cloned.1.call-start = ((), (), s32[]{:S(2)}) async-start(), calls=%async_computation.31 | async-start | bytes 2359296 | tf_op jit(solution)/shard_map/reduce_scatter | solution.py:290
  919.7 357.2 %reduce-scatter.31.cloned.1.call-start = ((), (), s32[]{:S(2)}) async-start(), calls=%async_computation.30 | async-start | bytes 2359296 | tf_op jit(solution)/shard_map/reduce_scatter | solution.py:287
  925.8 422.6 %reduce-scatter.29.cloned.1.call-start = ((), (), s32[]{:S(2)}) async-start(), calls=%async_computation.29 | async-start | bytes 2359296 | tf_op jit(solution)/shard_map/reduce_scatter | solution.py:284
  931.2 450.7 %reduce-scatter.27.cloned.1.call-start = ((), (), s32[]{:S(2)}) async-start(), calls=%async_computation.28 | async-start | bytes 2621440 | tf_op jit(solution)/shard_map/reduce_scatter | solution.py:269
  938.2 597.2 %reduce-scatter.41.cloned.1.call-start = ((), (), s32[]{:S(2)}) async-start(), calls=%async_computation.35 | async-start | bytes 9437184 | tf_op jit(solution)/shard_map/reduce_scatter | solution.py:311
  948.3 738.6 %reduce-scatter.39.cloned.1.call-start = ((), (), s32[]{:S(2)}) async-start(), calls=%async_computation.34 | async-start | bytes 9437184 | tf_op jit(solution)/shard_map/reduce_scatter | solution.py:308
  958.2 880.8 %reduce-scatter.37.cloned.1.call-start = ((), (), s32[]{:S(2)}) async-start(), calls=%async_computation.33 | async-start | bytes 9437184 | tf_op jit(solution)/shard_map/reduce_scatter | solution.py:305
  966.7 415.2 %copy-start.6 = (f32[128,2048]{1,0:T(8,128)S(1)}, f32[128,2048]{1,0:T(8,128)}, u32[]{:S(2)}) copy-start(f32[128,2048]{1,0:T(8,128)} %reduce-scatter.25.cloned.1.call-done) | copy-start | bytes 3145732
  (35 other events, 237.5 us)
Sparse Core Ops, SparseCore 0:
  9.6 25.2 all-gather.15
  37.0 49.2 all-gather.19
  88.5 47.7 all-gather.21
  138.3 47.7 all-gather.17
  188.0 49.5 all-gather.23
  242.6 42.6 reduce-scatter.20
  287.7 124.9 all-gather.27
  414.9 20.7 all-gather.25
  438.0 124.9 all-gather.29
  565.1 123.5 all-gather.31
  699.3 42.6 reduce-scatter.22
  747.5 22.5 all-gather.33
  800.3 44.4 reduce-scatter.24
  849.3 22.5 all-gather.35
  889.2 53.4 reduce-scatter.44
  946.6 52.5 reduce-scatter.42
  1003.3 60.9 reduce-scatter.46
  1067.7 67.3 reduce-scatter.34
  1138.7 67.4 reduce-scatter.32
  1209.5 67.2 reduce-scatter.30
  1280.9 67.3 reduce-scatter.28
  1351.4 30.4 reduce-scatter.26
  1386.0 149.3 reduce-scatter.40
  1538.9 148.0 reduce-scatter.38
  1691.0 147.9 reduce-scatter.36
where the time goes:
time: 1860 us; the launch traced here: 1850 us
  waiting for transfers between devices  1520 us (82%)
  matrix products  139 us (7%)
  blocking collectives  90.8 us (5%)
  other arithmetic  45.7 us (2%)
  local copies, waits for them, and re-layouts  32.5 us (2%)
    reduce_scatter x1, waiting for transfers between devices, local(): lax.psum_scatter(wgrad_down.astype(jnp.bfloat16), 'fsdp', scatter_dimensi...  151 us
    reduce_scatter x1, waiting for transfers between devices, local(): lax.psum_scatter(wgrad_gate.astype(jnp.bfloat16), 'fsdp', scatter_dimensi...  149 us
    reduce_scatter x1, waiting for transfers between devices, local(): lax.psum_scatter(wgrad_up.astype(jnp.bfloat16), 'fsdp', scatter_dimension...  149 us
    all_gather x1, waiting for transfers between devices, local(): lax.all_gather(w_gate, 'fsdp', axis=0, tiled=True)  122 us
    all_gather x1, waiting for transfers between devices, local(): lax.all_gather(w_up, 'fsdp', axis=0, tiled=True)  117 us
    all_gather x1, waiting for transfers between devices, local(): lax.all_gather(w_down, 'fsdp', axis=1, tiled=True)  115 us
    unnamed x28, waiting for transfers between devices  100 us
    reduce_scatter x1, waiting for transfers between devices, local(): lax.psum_scatter(wgrad_query.astype(jnp.bfloat16), 'fsdp', scatter_dimens...  69.6 us
  transfers between devices with their start and end apart: 25, of which 23 were waited for; matrix products, arithmetic and copies ran while one was open for 7% of the time, Pallas kernels for 0%

commit v1 on v0

v1 whole, which is shorter than its diff:
```python
import functools

import jax
import jax.numpy as jnp
import numpy as np
from jax import lax
from jax.experimental import pallas as pl
from jax.experimental.pallas import tpu as pltpu
from jax.sharding import PartitionSpec as P

HD = 128
NORM_EPS = 1e-06
ROPE_THETA = 500000.0
BF = jnp.bfloat16
F32 = jnp.float32
MIB = 1 << 20


class Place:
    def __init__(self, count):
        self.count = count
        self.outers = count // 4
        self.index = lax.axis_index("fsdp")
        self.tensor = lax.axis_index("tensor")
        self.low = self.index % 2
        self.high = self.index // 2
        self.pair = self.high % 2
        self.outer = self.high // 2
        self.core = self.tensor % 2
        self.side = self.tensor // 2

    def device(self, outer, pair, low, core, side):
        return {"fsdp": (outer * 2 + pair) * 2 + low, "tensor": side * 2 + core}

    def peer(self, pair=0, core=0, side=0):
        return self.device(
            self.outer, flip(self.pair, pair), self.low, flip(self.core, core), flip(self.side, side)
        )

    def slot(self, pair=0, core=0, side=0):
        return flip(self.pair, pair) * 4 + flip(self.core, core) * 2 + flip(self.side, side)

    def line(self, step, pair):
        outer = (self.outer + step) % self.outers
        return self.device(outer, flip(self.pair, pair), self.low, self.core, self.side)

    def high_at(self, step, pair):
        return ((self.outer + step + self.outers) % self.outers) * 2 + flip(self.pair, pair)

    def across(self):
        return self.device(self.outer, self.pair, 1 - self.low, self.core, self.side)

    def lines(self):
        return line_kinds(self.count)

    def group(self):
        return [(p, c, s) for p in (0, 1) for c in (0, 1) for s in (0, 1) if p or c or s]


def line_kinds(count):
    return [(step, pair) for step in reversed(range(count // 4)) for pair in (0, 1) if step or pair]


def flip(bit, yes):
    return 1 - bit if yes else bit


def greet(devices):
    barrier = pltpu.get_barrier_semaphore()
    for device in devices:
        pl.semaphore_signal(barrier, inc=1, device_id=device, device_id_type=pl.DeviceIdType.MESH)
    pl.semaphore_wait(barrier, len(devices))


def send(src, dst, sends, recvs, slot, device):
    return pltpu.make_async_remote_copy(
        src_ref=src,
        dst_ref=dst,
        send_sem=sends.at[slot],
        recv_sem=recvs.at[slot],
        device_id=device,
        device_id_type=pl.DeviceIdType.MESH,
    )


def product(left, right):
    return lax.dot_general(left, right, (((1,), (0,)), ((), ())), preferred_element_type=F32)


def product_last(left, right):
    return lax.dot_general(left, right, (((1,), (1,)), ((), ())), preferred_element_type=F32)


def product_first(left, right):
    return lax.dot_general(left, right, (((0,), (0,)), ((), ())), preferred_element_type=F32)


class Gather:
    slots = 9

    def __init__(self, place, rows, sends, recvs, split=False):
        half = rows.shape[1] // 2

        def go(slot, device, part=None, **kw):
            ref = rows.at[place.slot(**kw)]
            if part is not None:
                ref = rows.at[place.slot(**kw), pl.ds(part * half, half)]
            return send(ref, ref, sends, recvs, slot, place.peer(**device))

        self.to_pair = go(0, dict(pair=1))
        self.to_side = go(1, dict(side=1))
        self.to_core = go(2, dict(core=1))
        self.pair_to_core = go(5, dict(core=1), pair=1)
        self.side_to_core = go(6, dict(core=1), side=1)
        if split:
            self.relays = [go(3, dict(side=1), 0, pair=1), go(4, dict(pair=1), 1, side=1)]
            self.last = [go(7, dict(core=1), 0, pair=1, side=1), go(8, dict(core=1), 1, pair=1, side=1)]
        else:
            self.relays = [go(3, dict(side=1), pair=1)]
            self.last = [go(7, dict(core=1), pair=1, side=1)]

    def start(self):
        self.to_pair.start()
        self.to_side.start()
        self.to_core.start()

    def relay(self):
        self.to_pair.wait_recv()
        self.relays[0].start()
        self.pair_to_core.start()
        self.to_side.wait_recv()
        for copy in self.relays[1:]:
            copy.start()
        self.side_to_core.start()

    def finish(self):
        for relay, copy in zip(self.relays, self.last):
            relay.wait_recv()
            copy.start()
        for copy in [self.to_core, self.pair_to_core, self.side_to_core] + self.last:
            copy.wait_recv()

    def drain(self):
        for copy in [self.to_pair, self.to_side, self.to_core, self.pair_to_core, self.side_to_core]:
            copy.wait_send()
        for copy in self.relays + self.last:
            copy.wait_send()


class Scatter:
    order = [(1, 1), (1, 0), (0, 1), (0, 0)]

    def __init__(self, place, tile, parts, from_core, from_chips, total, sends, recvs, via=False):
        self.place, self.tile, self.parts = place, tile, parts
        self.from_core, self.from_chips, self.total, self.via = from_core, from_chips, total, via
        self.to_core = [
            send(
                parts.at[place.slot(pair=pair, core=1, side=side)],
                from_core.at[slot],
                sends,
                recvs,
                slot,
                place.peer(core=1),
            )
            for slot, (pair, side) in enumerate(self.order)
        ]
        self.to_chips = [
            send(
                parts.at[place.slot(pair=pair, side=side)],
                from_chips.at[slot],
                sends,
                recvs,
                4 + slot,
                place.peer(pair=pair if slot or not via else 0, side=side),
            )
            for slot, (pair, side) in enumerate(self.order[:3])
        ]

    def first(self, pair):
        place = self.place
        self.tile(flip(place.pair, pair), 1 - place.core)
        for slot, (p, side) in enumerate(self.order):
            if p == pair:
                self.to_core[slot].start()

    def both(self, slot):
        pair, side = self.order[slot]
        mine = self.place.slot(pair=pair, side=side)
        return mine, self.parts[mine].astype(F32) + self.from_core[slot].astype(F32)

    def second(self, pair):
        self.tile(flip(self.place.pair, pair), self.place.core)
        for slot, (p, side) in enumerate(self.order):
            if p != pair:
                continue
            self.to_core[slot].wait_recv()
            if self.via and slot == 1:
                continue
            mine, both = self.both(slot)
            if slot < 3:
                self.parts[mine] = both.astype(BF)
                self.to_chips[slot].start()
            else:
                self.total[...] = both

    def relay(self):
        if self.via:
            self.to_chips[0].wait_recv()
            mine, both = self.both(1)
            self.parts[mine] = (both + self.from_chips[0].astype(F32)).astype(BF)
            self.to_chips[1].start()

    def third(self):
        for slot, copy in enumerate(self.to_chips):
            if slot or not self.via:
                copy.wait_recv()
                self.total[...] += self.from_chips[slot].astype(F32)

    def drain(self):
        for copy in self.to_core + self.to_chips:
            copy.wait_send()


def tiles(left_ref, right, parts, lanes):
    own, width = parts.shape[1:]

    def tile(pair, core):
        first = pair * 4 + core * 2
        m = pl.ds(pl.multiple_of(first * own, 2 * own), 2 * own)

        @pl.loop(0, width // 256)
        def _(n):
            at = pl.ds(pl.multiple_of(n * 256, 256), 256)
            out = product_last(left_ref[m, :], right[at, lanes]).astype(BF)
            parts[first, :, at] = out[:own]
            parts[first + 1, :, at] = out[own:]

    return tile


def exchange_sums(place, stats, columns, sends, recvs):
    tokens = stats.shape[2]
    mine = place.slot()
    rows = [jnp.transpose(jnp.broadcast_to(column, (tokens, 128)))[0:1] for column in columns]
    stats[mine] = jnp.concatenate(rows + [jnp.zeros((6, tokens), F32)], axis=0)
    copies = []
    for i, (p, c, s) in enumerate(place.group()):
        copy = send(stats.at[mine], stats.at[mine], sends, recvs, i, place.peer(p, c, s))
        copy.start()
        copies.append(copy)
    return copies


def finish_sums(stats, copies):
    for copy in copies:
        copy.wait_recv()
    sums = stats[0]
    for g in range(1, 8):
        sums = sums + stats[g]
    return sums


def over_lanes(row):
    return jnp.transpose(jnp.broadcast_to(row, (128, row.shape[1])))


class Stream:
    def __init__(self, place, sources, full, sends, recvs, held, local):
        self.place = place
        self.kinds = sorted(place.lines())
        self.lines, self.over, self.hold, self.keep = [], [], [], []
        self.next = self.begun = self.begun_over = 0
        self.ahead, self.over_ahead = 1, 8
        depth = full.shape[1] // place.count
        per = place.count - 1
        for i, source in enumerate(sources):
            def rows(high, low, i=i):
                at = (high * 2 + low) * depth
                return full.at[i, pl.ds(pl.multiple_of(at, depth), depth)]

            own = rows(place.high, place.low)
            first = i * per
            self.lines.append(
                [
                    send(source(flip(place.pair, pair)), own, sends, recvs, first + k, place.line(step, pair))
                    for k, (step, pair) in enumerate(self.kinds)
                ]
            )
            first += len(self.kinds)
            over = [send(source(place.pair), own, sends, recvs, first, place.across())]
            for k, (step, pair) in enumerate(self.kinds):
                block = rows(place.high_at(-step, pair), place.low)
                over.append(send(block, block, sends, recvs, first + 1 + k, place.across()))
            self.over.append(over)
            self.hold.append(pltpu.make_async_copy(source(place.pair), held.at[i], local.at[0, i]))
            self.keep.append(pltpu.make_async_copy(held.at[i], own, local.at[1, i]))

    def place_own(self):
        for copy in self.hold:
            copy.start()
        for hold, keep in zip(self.hold, self.keep):
            hold.wait()
            keep.start()

    def fill(self):
        while self.begun < min(self.next // len(self.kinds) + self.ahead, len(self.lines)):
            for copy in self.lines[self.begun]:
                copy.start()
            self.begun += 1
        while self.begun_over < min(self.next // len(self.kinds) + self.over_ahead, len(self.lines)):
            self.over[self.begun_over][0].start()
            self.begun_over += 1

    def pump(self, number=1):
        per = len(self.kinds)
        for _ in range(number):
            i, k = divmod(self.next, per)
            if i >= len(self.lines):
                return
            self.lines[i][k].wait_recv()
            self.over[i][k + 1].start()
            self.next += 1
            if self.next % per == 0:
                self.fill()

    def arrive(self, i):
        self.pump(max(0, (i + 1) * len(self.kinds) - self.next))
        for copy in self.over[i]:
            copy.wait_recv()
        self.keep[i].wait()

    def drain(self):
        for copies in self.lines + self.over:
            for copy in copies:
                copy.wait_send()


ANY = pl.BlockSpec(memory_space=pl.ANY)
VMEM = pl.BlockSpec(memory_space=pltpu.VMEM)
DMA = pltpu.SemaphoreType.DMA


FORWARD_ORDER = (
    "k", "k", "k", "k", "k", "k", "xr", "k", "w2", "k", "xf", "t", "k", "k", "t", "k", "t", "q0",
    "k", "k", "q1", "q2", "s", "k", "k", "sf", "rope", "k", "k", "k", "k", "a", "a", "k", "k", "k",
    "k", "t", "f", "s1", "k", "k", "k", "k", "k", "s0", "rl", "k", "T", "k", "N", "k", "k", "R",
    "k", "k", "k", "k", "k", "G", "t", "g0", "k", "k", "k", "k", "g1", "t", "k", "k", "w2", "g2",
    "k", "k", "k", "t", "g3", "k", "t", "k", "t", "t",
)


def forward_kernel(
    count,
    rows_ref, q_ref, k_ref, v_ref, o_ref, gate_ref, up_ref, down_ref, gains_ref, tokens_ref, angles_ref, top_ref,
    full, gains_out, q_rot_out, k_rot_out, v_low_out, q_hat_out, k_hat_out, inv_out,
    normed_out, ainv_out, gate_out, up_out, output, part_out, probs_out, cos_out, sin_out, grad_out, mixed_turned, hidden_turned,
    rows_turned, mid_turned,
    all_rows, all_gains, gains, own_rows, att_w, ffn_w, raw, q_rot, k_rot, v_low, q_hat, k_hat, inv_ref,
    normed_ref, ainv_ref, gate_act, up_act, result, part_gain, probs_ref, cos_ref, sin_ref, mixed_t,
    bias_ref, token_rows, o_turned, down_turned, held,
    mixed, mid, hidden, turning, resid_ref, stats, parts, from_core, from_chips, total,
    wsends, wrecvs, keeps, loads, flushes, xsends, xrecvs, nsends, nrecvs, ssends, srecvs,
    rsends, rrecvs, gsends, grecvs, r2sends, r2recvs, g2sends, g2recvs, turn_sems, tsends, trecvs,
):
    place = Place(count)
    own, width = rows_ref.shape
    tokens = 8 * own
    big = tokens // 2
    cols = q_ref.shape[1] // 2
    heads = cols // HD
    mine = place.slot()
    others = [(place.index + step) % count for step in range(1, count)]

    first_copies = [
        pltpu.make_async_copy(rows_ref, all_rows.at[mine], loads.at[0]),
        pltpu.make_async_copy(gains_ref, all_gains.at[place.index], loads.at[1]),
        pltpu.make_async_copy(rows_ref, own_rows, loads.at[2]),
    ]
    for copy in first_copies:
        copy.start()
    turn_here = o_turned.shape[0] % 128 == 0
    if turn_here:
        narrow = [
            pltpu.make_async_copy(o_ref, ffn_w.at[pl.ds(0, o_ref.shape[0]), pl.ds(cols, cols)], loads.at[3]),
            pltpu.make_async_copy(down_ref, ffn_w.at[pl.ds(0, down_ref.shape[0]), pl.ds(0, cols)], loads.at[4]),
        ]
        for copy in narrow:
            copy.start()
    blocks = [side * 2 + core for core in (0, 1) for side in (0, 1)]
    token_rows[place.pair] = jnp.concatenate(
        [tokens_ref[:, block * own : (block + 1) * own] for block in blocks], axis=1
    )
    greet(
        [{"fsdp": other, "tensor": place.tensor} for other in others]
        + [place.peer(p, c, s) for p, c, s in place.group() if c or s]
    )
    token_copy = send(
        token_rows.at[place.pair], token_rows.at[place.pair], tsends, trecvs, 0, place.peer(pair=1)
    )
    token_copy.start()

    def pieces(ref):
        half = ref.shape[1] // 2

        def source(j):
            return lambda h: ref.at[:, pl.ds(pl.multiple_of(h * half + j * cols, cols), cols)]

        return [source(j) for j in range(half // cols)]

    o_source, down_source = (o_turned, down_turned) if turn_here else (o_ref, down_ref)
    gate_pieces, up_pieces = pieces(gate_ref), pieces(up_ref)
    sources = [pieces(ref)[0] for ref in (q_ref, k_ref, v_ref, o_source)]
    for pair in zip(gate_pieces, up_pieces):
        sources.extend(pair)
    sources.extend(pieces(down_source))
    steps = len(gate_pieces)
    stream = Stream(place, sources, full, wsends, wrecvs, held, keeps)
    rows_gather = Gather(place, all_rows, xsends, xrecvs)
    first_copies[0].wait()
    rows_gather.start()
    if turn_here:
        narrow[0].wait()
        o_turned[...] = jnp.transpose(ffn_w[: o_ref.shape[0], cols : 2 * cols])
        narrow[1].wait()
        for block in range(down_ref.shape[0] // 512):
            at = slice(block * 512, (block + 1) * 512)
            down_turned[:, at] = jnp.transpose(ffn_w[at, :cols])
    stream.fill()
    stream.place_own()
    first_copies[1].wait()
    gain_copies = []
    for i, other in enumerate(others):
        copy = send(
            all_gains.at[place.index],
            all_gains.at[place.index],
            nsends,
            nrecvs,
            i,
            {"fsdp": other, "tensor": place.tensor},
        )
        copy.start()
        gain_copies.append(copy)

    flushed = []

    def flush(src, dst):
        copy = pltpu.make_async_copy(src, dst, flushes.at[len(flushed)])
        copy.start()
        flushed.append(copy)

    token_copy.wait_recv()
    row = lax.broadcasted_iota(jnp.int32, (big, 128), 0)
    natural = row // own % 2 * (2 * own) + row // (2 * own) * own + row % own
    lane = lax.broadcasted_iota(jnp.int32, (big, 128), 1)
    for block in range(2):
        at = slice(block * big, (block + 1) * big)
        angle = over_lanes(token_rows[block, 0:1]) * angles_ref[0:1]
        cos_ref[at] = jnp.cos(angle)
        sin_ref[at] = jnp.sin(angle) * angles_ref[1:2]
        starts = over_lanes(token_rows[block, 1:2])
        for c in range(big // 128):
            lanes = slice(c * 128, (c + 1) * 128)
            first = c * 128
            key = first // own % 2 * (2 * own) + first // (2 * own) * own + first % own + lane
            allowed = (starts == token_rows[block, 1:2, lanes]) & (key <= natural)
            bias_ref[block, :, lanes] = jnp.where(allowed, 0.0, -1e30).astype(BF)
    flush(cos_ref, cos_out)
    flush(sin_ref, sin_out)

    turns = [(all_rows, rows_turned, block) for block in range(width // 512)]
    turns += [(mid, mid_turned, block) for block in range(width // 512)]
    turns += [(hidden, hidden_turned, block) for block in range(hidden.shape[1] // 512)]
    turned_copies = []

    def turn():
        n = len(turned_copies)
        ref, target, block = turns[n]
        if n >= 2:
            turned_copies[-2].wait()
        at = slice(block * 512, (block + 1) * 512)
        part = ref[:, :, at].reshape(tokens, 512) if len(ref.shape) == 3 else ref[:, at]
        turning[n % 2] = jnp.transpose(part)
        copy = pltpu.make_async_copy(turning.at[n % 2], target.at[at], turn_sems.at[n])
        copy.start()
        turned_copies.append(copy)

    def load(i, into):
        stream.arrive(i)
        copy = pltpu.make_async_copy(full.at[i], into, loads.at[5 + i])
        copy.start()
        return copy

    lanes_of = lambda c, number=1: pl.ds(c * cols, number * cols)
    wide = width // gains.shape[1]
    gain_row = lambda first: jnp.concatenate([gains[r : r + 1] for r in range(first, first + wide)], axis=1)

    def rows_arrive():
        rows_gather.finish()
        for copy in gain_copies:
            copy.wait_recv()
        sums = all_gains[0].astype(F32)
        for f in range(1, count):
            sums = sums + all_gains[f].astype(F32)
        gains[...] = sums
        flush(gains, gains_out)

    def project(which):
        load(which, att_w.at[:, lanes_of(which)]).wait()

        @pl.loop(0, 4)
        def _(i):
            m = pl.ds(pl.multiple_of(i * 2 * own, 2 * own), 2 * own)
            left = all_rows[pl.ds(i * 2, 2)].reshape(2 * own, width)
            raw[m, lanes_of(which)] = product(left, att_w[:, lanes_of(which)])

    sum_copies = []

    def squares():
        parts_of = [raw[:, at : at + cols] for at in (0, cols)]
        parts_of = [jnp.sum(part * part, axis=1, keepdims=True) for part in parts_of]
        sum_copies.extend(exchange_sums(place, stats, parts_of, ssends, srecvs))
        v_low[...] = raw[:, 2 * cols :].astype(BF)
        flush(v_low, v_low_out)

    def inverses():
        inverse = lax.rsqrt(finish_sums(stats, sum_copies) / width + NORM_EPS)
        inv_ref[0] = over_lanes(inverse[0:1])
        inv_ref[1] = over_lanes(inverse[1:2])
        flush(inv_ref, inv_out)

    def rotate():
        gain_at = pl.ds(pl.multiple_of(place.pair * cols, cols), cols)

        @pl.loop(0, 8)
        def _(i):
            m = pl.ds(pl.multiple_of(i * own, own), own)
            cosine = cos_ref[m]
            sine = sin_ref[m]
            for which, hat, rot in ((0, q_hat, q_rot), (1, k_hat, k_rot)):
                inv = inv_ref[which, m]
                gain = gains[2 * wide + which : 2 * wide + which + 1, gain_at]
                for h in range(heads):
                    lanes = slice(h * HD, (h + 1) * HD)
                    value = raw[m, which * cols + h * HD : which * cols + (h + 1) * HD] * inv
                    hat[m, lanes] = value
                    value = value * gain[:, lanes]
                    value = value * cosine + pltpu.roll(value, HD // 2, 1) * sine
                    rot[m, lanes] = value.astype(BF)

        for src, dst in ((q_rot, q_rot_out), (k_rot, k_rot_out), (q_hat, q_hat_out), (k_hat, k_hat_out)):
            flush(src, dst)

    scale = HD ** (-0.5)
    quarter = big // 2

    def attend(block, i):
        h = i // 2
        lanes = pl.ds(pl.multiple_of(h * HD, HD), HD)
        q_at = pl.ds(pl.multiple_of(block * big + i % 2 * quarter, quarter), quarter)
        k_at = pl.ds(pl.multiple_of(block * big, big), big)
        b_at = pl.ds(pl.multiple_of(i % 2 * quarter, quarter), quarter)
        scores = product_last(q_rot[q_at, lanes], k_rot[k_at, lanes]) * scale + bias_ref[block, b_at].astype(F32)
        top = jnp.max(scores, axis=1, keepdims=True)
        grown = jnp.exp(scores - top)
        probs = grown / jnp.sum(grown, axis=1, keepdims=True)
        probs = probs.astype(BF)
        probs_ref[block * heads + h, b_at] = probs
        mixed[q_at, lanes] = product(probs, v_low[k_at, lanes]).astype(BF)

    attended = [0]

    def attention():
        pl.loop(0, 2 * heads)(functools.partial(attend, attended[0]))
        attended[0] += 1

    tile = tiles(mixed, att_w, parts, lanes_of(3))
    scatter = Scatter(place, tile, parts, from_core, from_chips, total, rsends, rrecvs, via=True)
    gather = Gather(place, mid, gsends, grecvs)

    def out_first():
        out_load = load(3, att_w.at[:, lanes_of(3)])
        mixed_t[...] = jnp.transpose(mixed[...])
        flush(mixed_t, mixed_turned)
        flush(probs_ref, probs_out)
        rows_gather.drain()
        out_load.wait()
        scatter.first(1)
        scatter.first(0)

    def norm():
        araw = total[...]
        inv = lax.rsqrt(jnp.mean(araw * araw, axis=1, keepdims=True) + NORM_EPS)
        normed = araw * inv
        normed_ref[...] = normed
        ainv_ref[...] = jnp.broadcast_to(inv, (own, 128))
        first_copies[2].wait()
        resid = own_rows[...].astype(F32) + normed * gain_row(0)
        resid_ref[...] = resid
        mid[mine] = resid.astype(BF)
        gather.start()
        for src, dst in ((normed_ref, normed_out), (ainv_ref, ainv_out)):
            flush(src, dst)

    loaded = {}

    def load_step(j):
        if j < steps and j not in loaded:
            at = j % 2 * 2
            loaded[j] = [load(4 + 2 * j + r, ffn_w.at[:, lanes_of(at + r)]) for r in range(2)]

    def gate_and_up(j):
        load_step(j)
        for copy in loaded[j]:
            copy.wait()
        n = slice(j * cols, (j + 1) * cols)

        @pl.loop(0, 4)
        def _(i):
            m = pl.ds(pl.multiple_of(i * 2 * own, 2 * own), 2 * own)
            left = mid[pl.ds(i * 2, 2)].reshape(2 * own, width)
            both = product(left, ffn_w[:, lanes_of(j % 2 * 2, 2)])
            gate = both[:, :cols]
            up = both[:, cols:]
            sig = jax.nn.sigmoid(gate)
            silu = gate * sig
            gate_act[m, n] = up * sig * (1.0 + gate * (1.0 - sig))
            up_act[m, n] = silu
            hidden[m, n] = (silu * up).astype(BF)

        if j == steps - 1:
            for src, dst in ((gate_act, gate_out), (up_act, up_out)):
                flush(src, dst)

    actions = {
        "k": stream.pump,
        "t": turn,
        "xr": rows_gather.relay,
        "xf": rows_arrive,
        "q0": lambda: project(0),
        "q1": lambda: project(1),
        "q2": lambda: project(2),
        "s": squares,
        "sf": inverses,
        "rope": rotate,
        "a": attention,
        "f": out_first,
        "s1": lambda: scatter.second(1),
        "s0": lambda: scatter.second(0),
        "rl": scatter.relay,
        "T": scatter.third,
        "N": norm,
        "R": gather.relay,
        "G": gather.finish,
    }
    for j in range(steps):
        actions["g%d" % j] = functools.partial(gate_and_up, j)
    each = len(stream.kinds) // 3
    for name in FORWARD_ORDER:
        if name == "k":
            stream.pump(each)
        elif name[0] == "w":
            stream.ahead = int(name[1:])
            stream.fill()
        else:
            actions[name]()

    downs = [
        load(i, att_w.at[:, lanes_of(j)]) for j, i in enumerate(range(4 + 2 * steps, len(sources)))
    ]
    for copy in downs:
        copy.wait()
    scatter.drain()
    tile = tiles(hidden, att_w, parts, lanes_of(0, steps))
    again = Scatter(place, tile, parts, from_core, from_chips, total, r2sends, r2recvs)
    again.first(1)
    again.first(0)
    again.second(1)
    again.second(0)
    top = top_ref[...].astype(F32)
    gain = gain_row(wide)
    again.third()
    fraw = total[...]
    inv = lax.rsqrt(jnp.mean(fraw * fraw, axis=1, keepdims=True) + NORM_EPS)
    normed = fraw * inv
    scaled = top * gain
    inner = jnp.mean(scaled * normed, axis=1, keepdims=True)
    all_rows[mine] = (inv * (scaled - normed * inner)).astype(BF)
    last = Gather(place, all_rows, g2sends, g2recvs, split=True)
    last.start()
    result[...] = (resid_ref[...] + normed * gain).astype(BF)
    part_gain[...] = jnp.broadcast_to(jnp.sum(top * normed, axis=0, keepdims=True), part_gain.shape)
    flush(result, output)
    flush(part_gain, part_out)
    last.relay()
    stream.drain()
    gather.drain()
    again.drain()
    for copy in sum_copies + gain_copies + [token_copy]:
        copy.wait_send()
    last.finish()
    flush(all_rows, grad_out)
    last.drain()
    for copy in flushed + turned_copies[-2:]:
        copy.wait()


def run_forward(count, rows, wq, wk, wv, wo, gate, up, down, gains, token_rows, angles, top):
    own, width = rows.shape
    tokens = 8 * own
    half = gate.shape[1] // 2
    cols = wq.shape[1] // 2
    depth = width // count
    pieces = 4 + 3 * (half // cols)
    per = pieces * (count - 1)
    shape = jax.ShapeDtypeStruct
    outs = (
        shape((pieces, width, cols), BF),
        shape(gains.shape, F32),
        shape((tokens, cols), BF), shape((tokens, cols), BF), shape((tokens, cols), BF),
        shape((tokens, cols), F32), shape((tokens, cols), F32), shape((2, tokens, 128), F32),
        shape((own, width), F32), shape((own, 128), F32),
        shape((tokens, half), F32), shape((tokens, half), F32),
        shape((own, width), BF), shape((8, width), F32), shape((2 * cols // HD, tokens // 2, tokens // 2), BF),
        shape((tokens, 128), F32), shape((tokens, 128), F32),
        shape((8, own, width), BF),
        shape((cols, tokens), BF), shape((half, tokens), BF), shape((width, tokens), BF), shape((width, tokens), BF),
    )
    scratch = lambda out: pltpu.VMEM(out.shape, out.dtype)
    return pl.pallas_call(
        functools.partial(forward_kernel, count),
        out_shape=outs,
        in_specs=[ANY] * 9 + [VMEM] * 3,
        out_specs=[ANY] * len(outs),
        scratch_shapes=[
            pltpu.VMEM((8, own, width), BF),
            pltpu.VMEM((count,) + gains.shape, BF),
            scratch(outs[1]),
            pltpu.VMEM((own, width), BF),
            pltpu.VMEM((width, max(4 * cols, half)), BF),
            pltpu.VMEM((width, 4 * cols), BF),
            pltpu.VMEM((tokens, 3 * cols), F32),
            *[scratch(out) for out in outs[2:-5]],
            scratch(outs[-4]),
            pltpu.VMEM((2, tokens // 2, tokens // 2), BF),
            pltpu.VMEM((2,) + token_rows.shape, F32),
            pltpu.VMEM((depth, 2 * cols), BF),
            pltpu.VMEM((depth, 2 * half), BF),
            pltpu.VMEM((pieces, depth, cols), BF),
            pltpu.VMEM((tokens, cols), BF),
            pltpu.VMEM((8, own, width), BF),
            pltpu.VMEM((tokens, half), BF),
            pltpu.VMEM((2, 512, tokens), BF),
            pltpu.VMEM((own, width), F32),
            pltpu.VMEM((8, 8, tokens), F32),
            pltpu.VMEM((8, own, width), BF),
            pltpu.VMEM((4, own, width), BF),
            pltpu.VMEM((3, own, width), BF),
            pltpu.VMEM((own, width), F32),
            DMA((per,)), DMA((per,)), DMA((2, pieces)), DMA((5 + pieces,)), DMA((len(outs),)),
            DMA((9,)), DMA((9,)),
            DMA((count - 1,)), DMA((count - 1,)),
            DMA((7,)), DMA((7,)),
            DMA((7,)), DMA((7,)),
            DMA((9,)), DMA((9,)),
            DMA((7,)), DMA((7,)),
            DMA((9,)), DMA((9,)),
            DMA((2 * (width // 512) + half // 512,)),
            DMA((1,)), DMA((1,)),
        ],
        compiler_params=pltpu.CompilerParams(
            collective_id=0, has_side_effects=True, vmem_limit_bytes=62 * MIB
        ),
        name="forward",
    )(rows, wq, wk, wv, wo, gate, up, down, gains, token_rows, angles, top)


COLUMN_MATRICES = (0, 3)

ORDER = (
    "d", "d", "A", "d", "f1", "p", "f0", "s1", "d", "p", "s0", "d", "p", "d", "d", "p", "d", "d",
    "p", "T", "N", "p", "d", "p", "R", "d", "p", "d", "p", "G", "D", "a", "a", "d", "r", "p", "d",
    "q", "F1", "d", "F0", "d", "p", "d", "S1", "p", "p", "p", "p", "d", "d", "p", "d", "S0", "p",
    "p", "d", "p", "d", "p", "p", "d", "p", "d", "p", "T2", "p",
)


class Collect:
    def __init__(self, place, pieces, depth, gbuf, ybuf, zbuf, ring, came, have, ready, kept, local, ysends,
                 yrecvs, zsends, zrecvs, loads, keeps):
        self.place, self.pieces, self.depth = place, pieces, depth
        columns = [matrix in COLUMN_MATRICES for matrix, _, _, _ in pieces]
        at = [columns[:p].count(columns[p]) for p in range(len(pieces))]
        self.gbuf, self.ybuf, self.zbuf = (
            [bufs[columns[p]].at[at[p]] for p in range(len(pieces))] for bufs in (gbuf, ybuf, zbuf)
        )
        self.ring = ring
        self.came, self.have, self.ready, self.kept = came, have, ready, kept
        self.loads, self.settled = loads, []
        self.made = self.launched = self.summed = 0
        self.flying = []
        self.local, self.over, self.line, self.keep = [], [], [], []
        slot = 0
        for p, (matrix, rows, wide, kind) in enumerate(pieces):
            box = (pl.ds(0, rows), pl.ds(0, wide))
            self.local.append(
                pltpu.make_async_copy(ring.at[(p % 2, slice(None)) + box], self.gbuf[p].at[(slice(None),) + box], local.at[p])
            )
            self.over.append(
                send(
                    self.gbuf[p].at[(1 - place.low,) + box],
                    self.ybuf[p].at[box],
                    ysends,
                    yrecvs,
                    p,
                    place.across(),
                )
            )
            self.keep.append(
                pltpu.make_async_copy(self.gbuf[p].at[(place.low,) + box], have.at[box], loads.at[0])
            )
            if kind == (0, 0):
                self.line.append(None)
                self.settled.append(
                    pltpu.make_async_copy(kept[matrix], self.zbuf[p].at[box], keeps.at[len(self.settled)])
                )
                continue
            self.line.append(
                send(
                    ready.at[(slot % ready.shape[0],) + box],
                    self.zbuf[p].at[box],
                    zsends,
                    zrecvs,
                    p,
                    place.line(*kind),
                )
            )
            slot += 1

    def owner(self, p):
        both = 2 * self.depth
        return pl.ds(pl.multiple_of(self.place.high_at(*self.pieces[p][3]) * both, both), both)

    def make_rows(self, left, right, first):
        p = self.made
        self.launch()
        ring = self.ring.at[p % 2]
        wide = self.pieces[p][2]
        step = 256

        @pl.loop(0, wide // step)
        def _(n):
            lanes = pl.ds(pl.multiple_of(first + n * step, step), step)
            to = pl.ds(pl.multiple_of(n * step, step), step)
            for low in (0, 1):
                rows = left[low * self.depth : (low + 1) * self.depth]
                ring[low, : self.depth, to] = product(rows, right[:, lanes]).astype(BF)

        self.local[p].start()
        self.made = p + 1

    def make_columns(self, left, right):
        p = self.made
        self.launch()
        ring = self.ring.at[p % 2]
        _, rows, wide, _ = self.pieces[p]
        number = left.shape[0] // rows
        pitch = wide // number
        tokens = right.shape[0] * right.shape[1]
        cols = right[:, :, self.owner(p)].reshape(tokens, 2 * self.depth)
        for c in range(number):
            out = product(left[c * rows : (c + 1) * rows], cols).astype(BF)
            for low in (0, 1):
                ring[low, :rows, c * pitch : c * pitch + self.depth] = out[
                    :, low * self.depth : (low + 1) * self.depth
                ]
        self.local[p].start()
        self.made = p + 1

    def launch(self):
        while self.launched < self.made:
            self.local[self.launched].wait()
            self.over[self.launched].start()
            self.launched += 1

    def pump(self, number=1):
        self.launch()
        for _ in range(number):
            p = self.summed
            if p >= self.made:
                return
            matrix, rows, wide, kind = self.pieces[p]
            box = (slice(0, rows), slice(0, wide))
            self.keep[p].start()
            self.over[p].wait_recv()
            came = pltpu.make_async_copy(
                self.ybuf[p].at[pl.ds(0, rows), pl.ds(0, wide)],
                self.came.at[pl.ds(0, rows), pl.ds(0, wide)],
                self.loads.at[2],
            )
            came.start()
            self.keep[p].wait()
            came.wait()
            total = self.came[box].astype(F32) + self.have[box].astype(F32)
            if kind == (0, 0):
                self.kept[matrix][...] = total.astype(BF)
                self.settled[matrix].start()
            else:
                slots = self.ready.shape[0]
                if len(self.flying) >= slots:
                    self.flying[-slots].wait_send()
                self.ready[(len(self.flying) % slots,) + box] = total.astype(BF)
                self.line[p].start()
                self.flying.append(self.line[p])
            self.summed = p + 1

    def drain(self):
        for copy in self.over:
            copy.wait_send()
        for copy in self.flying[-self.ready.shape[0] :]:
            copy.wait_send()
        for copy in self.line:
            if copy is not None:
                copy.wait_recv()
        for copy in self.settled:
            copy.wait()


def backward_kernel(
    count, pieces,
    gffn_in, hidden_in, gate_in, up_in, mid_in, rows_in, full, mixed_in, q_in, k_in, v_in, qh_in, kh_in, inv_in,
    cos_in, sin_in, probs_in, normed_ref, ainv_ref, top_ref, gains_ref, pgain_ref,
    grad_rows, gain_sums,
    gbuf_r, gbuf_c, ybuf_r, ybuf_c, zbuf_r, zbuf_c,
    rows_a, rows_c, hidden, acts, floats, weights, parts, from_core, from_chips, total, resid, turned, ring,
    came, have, ready, kept0, kept1, kept2, kept3, kept4, kept5,
    mixed, q_rot, k_rot, v_low, q_hat, k_hat, inv, cos_ref, sin_ref, probs_ref, datt, dqkv, stats, side_sums, all_sums,
    big_loads, loads, local, ysends, yrecvs, zsends, zrecvs, rsends, rrecvs, r2sends, r2recvs, gsends, grecvs,
    ssends, srecvs, xsends, xrecvs, fsends, frecvs, keeps,
):
    place = Place(count)
    own, width = top_ref.shape
    tokens = 8 * own
    big = tokens // 2
    cols = mixed.shape[0]
    heads = cols // HD
    steps = hidden.shape[0] // cols
    depth = width // count
    others = [(place.index + step) % count for step in range(1, count)]
    tensor_peers = [(0, 1), (1, 0), (1, 1)]

    used = [0]

    def load(src, into):
        copy = pltpu.make_async_copy(src, into, big_loads.at[used[0]])
        used[0] += 1
        copy.start()
        return copy

    def chunk(ref, j):
        return ref.at[:, pl.ds(j * cols, cols)]

    rows_load = load(gffn_in, rows_a)
    hidden_load = load(hidden_in, hidden)
    firsts = [
        [
            load(full.at[4 + 2 * steps + j], chunk(weights, j)),
            load(chunk(gate_in, j), floats.at[2 * (j % 2)]),
            load(chunk(up_in, j), floats.at[2 * (j % 2) + 1]),
        ]
        for j in range(min(2, steps))
    ]
    for j in range(2, steps):
        firsts.append([load(full.at[4 + 2 * steps + j], chunk(weights, j))])
    greet(
        [{"fsdp": other, "tensor": place.tensor} for other in others]
        + [place.peer(p, c, s) for p, c, s in place.group() if c or s]
    )
    kept = [kept0, kept1, kept2, kept3, kept4, kept5]
    collect = Collect(
        place, pieces, depth, (gbuf_r, gbuf_c), (ybuf_r, ybuf_c), (zbuf_r, zbuf_c), ring, came, have, ready, kept, local,
        ysends, yrecvs, zsends, zrecvs, loads, keeps,
    )
    number = len(place.lines()) + 1

    wanted = [(mid_in, number + 2 * k) for k in range(number)] + [
        (rows_in, (4 + turn) * number + k) for turn in range(2) for k in range(number)
    ]
    blocks = []

    def next_block():
        i = len(blocks)
        if i < len(wanted):
            ref, p = wanted[i]
            blocks.append(load(ref.at[collect.owner(p)], turned.at[i % 2]))

    next_block()
    next_block()
    waited = set()

    def once(*copies):
        for copy in copies:
            if id(copy) not in waited:
                waited.add(id(copy))
                copy.wait()

    def make_down():
        once(rows_load, hidden_load)
        collect.make_columns(hidden, rows_a)

    def make_rows(i, right, first, last):
        once(blocks[i])
        collect.make_rows(turned.at[i % 2], right, first)
        if last:
            next_block()

    makes = [make_down] * number
    for k in range(number):
        makes.append(functools.partial(make_rows, k, acts, 0, False))
        makes.append(functools.partial(make_rows, k, acts, steps * cols, True))
    def make_out():
        once(*late["rest"])
        collect.make_columns(mixed, rows_c)

    makes += [make_out] * number
    for turn, first in ((1, 2 * cols), (2, 0)):
        for k in range(number):
            makes.append(functools.partial(make_rows, turn * number + k, dqkv, first, True))

    late = {}

    def gate_and_up():
        once(rows_load)
        for j in range(steps):
            once(*firsts[j])
            at = 2 * (j % 2)

            @pl.loop(0, 4)
            def _(i):
                m = pl.ds(pl.multiple_of(i * 2 * own, 2 * own), 2 * own)
                left = rows_a[pl.ds(i * 2, 2)].reshape(2 * own, width)
                grad = product(left, weights[:, j * cols : (j + 1) * cols])
                acts[m, 2 * j * cols : (2 * j + 1) * cols] = (grad * floats[at, m]).astype(BF)
                acts[m, (2 * j + 1) * cols : (2 * j + 2) * cols] = (grad * floats[at + 1, m]).astype(BF)

            if j + 2 < steps:
                firsts[j + 2] += [
                    load(chunk(gate_in, j + 2), floats.at[at]),
                    load(chunk(up_in, j + 2), floats.at[at + 1]),
                ]
        late["ffn"] = [load(full.at[4 + c], chunk(weights, c)) for c in range(2 * steps)]
        late["rest"] = [
            load(src, into)
            for src, into in (
                (mixed_in, mixed), (q_in, q_rot), (k_in, k_rot), (v_in, v_low), (qh_in, q_hat), (kh_in, k_hat),
                (inv_in, inv), (cos_in, cos_ref), (sin_in, sin_ref), (probs_in, probs_ref),
            )
        ]

    tile = tiles(acts, weights, parts, pl.ds(0, acts.shape[1]))
    scatter = Scatter(place, tile, parts, from_core, from_chips, total, rsends, rrecvs, via=True)
    tile = tiles(dqkv, weights, parts, pl.ds(0, 3 * cols))
    again = Scatter(place, tile, parts, from_core, from_chips, total, r2sends, r2recvs, via=True)
    gather = Gather(place, rows_c, gsends, grecvs)
    wide = width // gains_ref.shape[1]
    lanes_per = gains_ref.shape[1]
    cut = lambda row: [row[:, r * lanes_per : (r + 1) * lanes_per] for r in range(wide)]
    side_copies, inner_copies, all_copies = [], [], []

    def first(pair):
        once(*late["ffn"])
        scatter.first(pair)

    def second(pair):
        scatter.second(pair)
        if not pair:
            scatter.relay()
            late["att"] = [load(full.at[c], chunk(weights, c)) for c in range(4)]

    def norm():
        normed = normed_ref[...]
        gain = jnp.concatenate([gains_ref[r : r + 1] for r in range(wide)], axis=1)
        grad = top_ref[...].astype(F32) + total[...]
        resid[...] = grad
        part_gain = jnp.sum(grad * normed, axis=0, keepdims=True)
        scaled = grad * gain
        inner = jnp.mean(scaled * normed, axis=1, keepdims=True)
        rows_c[place.slot()] = (ainv_ref[:, :1] * (scaled - normed * inner)).astype(BF)
        gather.start()
        side_sums[place.tensor] = jnp.concatenate(cut(part_gain) + cut(pgain_ref[0:1]), axis=0)
        for i, (c, s) in enumerate(tensor_peers):
            copy = send(
                side_sums.at[place.tensor], side_sums.at[place.tensor], xsends, xrecvs, i, place.peer(0, c, s)
            )
            copy.start()
            side_copies.append(copy)

    def out_back():
        once(*late["att"], *late["rest"])

        @pl.loop(0, 4)
        def _(i):
            m = pl.ds(pl.multiple_of(i * 2 * own, 2 * own), 2 * own)
            left = rows_c[pl.ds(i * 2, 2)].reshape(2 * own, width)
            datt[m] = product(left, weights[:, 3 * cols : 4 * cols]).astype(BF)

    scale = HD ** (-0.5)
    quarter = big // 2

    def attend(block, h):
        lanes = pl.ds(pl.multiple_of(h * HD, HD), HD)
        k_at = pl.ds(pl.multiple_of(block * big, big), big)
        keys = k_rot[k_at, lanes]
        values = v_low[k_at, lanes]
        for half in range(2):
            q_at = pl.ds(pl.multiple_of(block * big + half * quarter, quarter), quarter)
            queries = q_rot[q_at, lanes]
            grads = datt[q_at, lanes]
            low = probs_ref[block * heads + h, half * quarter : (half + 1) * quarter]
            probs = low.astype(F32)
            dprobs = product_last(grads, values)
            inner = jnp.sum(probs * dprobs, axis=1, keepdims=True)
            dscores = (probs * (dprobs - inner)).astype(BF)
            floats[0, q_at, lanes] = product(dscores, keys) * scale
            dkeys = product_first(dscores, queries) * scale
            dvalues = product_first(low, grads)
            if half:
                floats[1, k_at, lanes] += dkeys
                floats[2, k_at, lanes] += dvalues
            else:
                floats[1, k_at, lanes] = dkeys
                floats[2, k_at, lanes] = dvalues

    attended = [0]

    def attention():
        pl.loop(0, heads)(functools.partial(attend, attended[0]))
        m = pl.ds(attended[0] * big, big)
        dqkv[m, 2 * cols :] = floats[2, m].astype(BF)
        attended[0] += 1

    def rotate_back():
        gain_at = pl.ds(pl.multiple_of(place.pair * cols, cols), cols)
        norm_gains = [gains_ref[2 * wide + which : 2 * wide + which + 1, gain_at] for which in (0, 1)]
        gain_parts, inners = [], []
        for which, hat in ((0, q_hat), (1, k_hat)):
            pieces_of = []
            for h in range(heads):
                lanes = slice(h * HD, (h + 1) * HD)
                value = floats[which, :, lanes]
                value = value * cos_ref[...] - pltpu.roll(value, HD // 2, 1) * sin_ref[...]
                weighted = value * hat[:, lanes]
                gain_parts.append(jnp.sum(weighted, axis=0, keepdims=True))
                part = norm_gains[which][:, lanes]
                pieces_of.append(jnp.sum(weighted * part, axis=1, keepdims=True))
                floats[which, :, lanes] = value * part
            inners.append(sum(pieces_of[1:], pieces_of[0]))
        inner_copies.extend(exchange_sums(place, stats, inners, ssends, srecvs))
        for copy in side_copies:
            copy.wait_recv()
        side = side_sums[0]
        for t in range(1, side_sums.shape[0]):
            side = side + side_sums[t]
        gain_rows = [jnp.concatenate(gain_parts[w * heads : (w + 1) * heads], axis=1) for w in (0, 1)]
        upper = place.pair == 1
        gain_rows = [
            jnp.concatenate([jnp.where(upper, 0.0, row), jnp.where(upper, row, 0.0)], axis=1) for row in gain_rows
        ]
        spare = jnp.zeros((all_sums.shape[1] - 2 * wide - 2, lanes_per), F32)
        all_sums[place.index] = jnp.concatenate([side] + gain_rows + [spare], axis=0)
        for i, other in enumerate(others):
            copy = send(
                all_sums.at[place.index], all_sums.at[place.index], fsends, frecvs, i,
                {"fsdp": other, "tensor": place.tensor},
            )
            copy.start()
            all_copies.append(copy)

    def query_key():
        sums = finish_sums(stats, inner_copies) / width
        for which, hat in ((0, q_hat), (1, k_hat)):
            lanes_inner = over_lanes(sums[which : which + 1])
            for h in range(heads):
                lanes = slice(h * HD, (h + 1) * HD)
                value = inv[which] * (floats[which, :, lanes] - hat[:, lanes] * lanes_inner)
                dqkv[:, which * cols + h * HD : which * cols + (h + 1) * HD] = value.astype(BF)

    def first_again(pair):
        if pair:
            scatter.drain()
        again.first(pair)

    def second_again(pair):
        again.second(pair)
        if not pair:
            again.relay()

    grad_copies = []

    def third_again():
        again.third()
        total[...] += resid[...]
        grad_copies.append(load(total, grad_rows))

    actions = {
        "A": gate_and_up,
        "f1": lambda: first(1),
        "f0": lambda: first(0),
        "s1": lambda: second(1),
        "s0": lambda: second(0),
        "T": scatter.third,
        "N": norm,
        "R": gather.relay,
        "G": gather.finish,
        "D": out_back,
        "a": attention,
        "r": rotate_back,
        "q": query_key,
        "F1": lambda: first_again(1),
        "F0": lambda: first_again(0),
        "S1": lambda: second_again(1),
        "S0": lambda: second_again(0),
        "T2": third_again,
    }
    each = number // 4
    for name in ORDER:
        if name == "d":
            for _ in range(each):
                makes.pop(0)()
        elif name == "p":
            collect.pump(each)
        else:
            actions[name]()
    for copy in all_copies:
        copy.wait_recv()
    sums = all_sums[0]
    for f in range(1, count):
        sums = sums + all_sums[f]
    gain_sums[...] = sums
    for copy in grad_copies:
        copy.wait()
    collect.drain()
    again.drain()
    gather.drain()
    for copy in inner_copies + side_copies + all_copies:
        copy.wait_send()


def list_pieces(count, depth, cols, half):
    kinds = line_kinds(count) + [(0, 0)]
    pitch = max(depth, 128)
    sizes = [
        (cols, half // cols * pitch), (depth, half), (depth, half), (cols, pitch), (depth, cols), (depth, 2 * cols),
    ]
    order = [[0], [1, 2], [3], [4], [5]]
    return sizes, [(m,) + sizes[m] + (kind,) for group in order for kind in kinds for m in group]


def settle_kernel(
    pieces, zbuf_r, zbuf_c, grad_in, out_in,
    out_q, out_k, out_v, out_o, out_gate, out_up, out_down, grad_out, out_out,
    boxes_r, boxes_c, grad_held, out_held, stage0, stage1, stage2, stage3, stage4, stage5, loads, stores, copies,
):
    stages = [stage0, stage1, stage2, stage3, stage4, stage5]
    whole = []
    for i, (src, held_here, dst) in enumerate(((grad_in, grad_held, grad_out), (out_in, out_held, out_out))):
        into = pltpu.make_async_copy(src, held_here, copies.at[i])
        into.start()
        whole.append((into, pltpu.make_async_copy(held_here, dst, copies.at[2 + i])))
    pair = lax.axis_index("fsdp") // 2 % 2
    held, count = [], [0, 0]
    for p, (matrix, _, _, _) in enumerate(pieces):
        column = matrix in COLUMN_MATRICES
        at = count[column]
        count[column] += 1
        zbuf, boxes = (zbuf_c, boxes_c) if column else (zbuf_r, boxes_r)
        _, rows, wide, _ = pieces[p]
        box = (pl.ds(0, rows), pl.ds(0, wide))
        copy = pltpu.make_async_copy(zbuf.at[(at,) + box], boxes.at[(at,) + box], loads.at[p])
        copy.start()
        held.append((copy, boxes, at))
    for into, back in whole:
        into.wait()
        back.start()
    cols = out_q.shape[1] // 2
    steps = out_gate.shape[1] // 2 // cols
    both = [(ref, j * cols) for j in range(steps) for ref in (out_gate, out_up)]
    groups = [
        [(out_down, None)] * steps,
        both[:steps],
        both[steps:],
        [(out_o, None)],
        [(out_v, 0)],
        [(out_q, 0), (out_k, 0)],
    ]
    sent = []
    for matrix, targets in enumerate(groups):
        for p, (m, _, _, _) in enumerate(pieces):
            if m == matrix:
                held[p][0].wait()
        stage = stages[matrix]
        rows, wide = stage.shape[1:]
        step = min(rows, 64)

        @pl.loop(0, rows // step)
        def _(i):
            at = pl.ds(pl.multiple_of(i * step, step), step)
            sums = [None, None]
            for p, (m, _, _, kind) in enumerate(pieces):
                if m != matrix:
                    continue
                _, boxes, index = held[p]
                part = boxes[index, at, :wide].astype(F32)
                which = kind[1]
                sums[which] = part if sums[which] is None else sums[which] + part
            stage[0, at] = sums[0]
            stage[1, at] = sums[1]

        pitch = wide // len(targets)
        for r in (0, 1):
            half = flip(pair, r)
            for c, (ref, at) in enumerate(targets):
                src = stage.at[r, :, pl.ds(c * pitch, pitch)]
                if at is None:
                    start = half * (ref.shape[0] // 2) + c * rows
                    dst = ref.at[pl.ds(pl.multiple_of(start, rows), rows)]
                else:
                    start = half * (ref.shape[1] // 2) + at
                    dst = ref.at[:, pl.ds(pl.multiple_of(start, pitch), pitch)]
                copy = pltpu.make_async_copy(src, dst, stores.at[len(sent)])
                copy.start()
                sent.append(copy)
    for copy in sent + [back for _, back in whole]:
        copy.wait()


def run_settle(count, cols, half, zbuf_r, zbuf_c, grad, output):
    width = grad.shape[1]
    depth = width // count
    sizes, pieces = list_pieces(count, depth, cols, half)
    pitch = max(depth, 128)
    shape = jax.ShapeDtypeStruct
    small = shape((depth, 2 * cols), F32)
    large = shape((depth, 2 * half), F32)
    outs = (
        small, small, small, shape((2 * cols, pitch), F32),
        large, large, shape((2 * half, pitch), F32),
        shape(grad.shape, grad.dtype), shape(output.shape, output.dtype),
    )
    return pl.pallas_call(
        functools.partial(settle_kernel, pieces),
        out_shape=outs,
        in_specs=[ANY] * 4,
        out_specs=[ANY] * len(outs),
        scratch_shapes=[
            pltpu.VMEM(zbuf_r.shape, BF),
            pltpu.VMEM(zbuf_c.shape, BF),
            pltpu.VMEM(grad.shape, grad.dtype),
            pltpu.VMEM(output.shape, output.dtype),
            *[pltpu.VMEM((2,) + size, F32) for size in sizes],
            DMA((len(pieces),)), DMA((64,)), DMA((4,)),
        ],
        compiler_params=pltpu.CompilerParams(vmem_limit_bytes=62 * MIB),
        name="settle",
    )(zbuf_r, zbuf_c, grad, output)


def run_backward(
    count, gffn, hidden, gate, up, mid, rows, full, mixed, q_rot, k_rot, v_low, q_hat, k_hat, inv, cosine, sine, probs,
    normed, ainv, top, gains, part_gain,
):
    own, width = top.shape
    tokens = 8 * own
    cols = mixed.shape[0]
    half = hidden.shape[0]
    depth = width // count
    steps = half // cols
    pitch = max(depth, 128)
    kinds = line_kinds(count) + [(0, 0)]
    sizes, pieces = list_pieces(count, depth, cols, half)
    number = len(pieces)
    kinds_of = ((4 * len(kinds), sizes[1]), (2 * len(kinds), sizes[0]))
    box = (max(depth, cols), half)
    shape = jax.ShapeDtypeStruct
    outs = (
        shape((own, width), F32),
        shape(gains.shape, F32),
        *[shape((n,) + lead + size, BF) for lead in ((2,), (), ()) for n, size in kinds_of],
    )
    like = lambda array: pltpu.VMEM(array.shape, array.dtype)
    return pl.pallas_call(
        functools.partial(backward_kernel, count, pieces),
        out_shape=outs,
        in_specs=[ANY] * 17 + [VMEM] * 5,
        out_specs=[ANY, VMEM] + [ANY] * 6,
        scratch_shapes=[
            like(gffn), like(gffn), like(hidden),
            pltpu.VMEM((tokens, 2 * half), BF),
            pltpu.VMEM((4, tokens, cols), F32),
            pltpu.VMEM((width, 2 * half), BF),
            pltpu.VMEM((8, own, width), BF),
            pltpu.VMEM((4, own, width), BF),
            pltpu.VMEM((3, own, width), BF),
            pltpu.VMEM((own, width), F32),
            pltpu.VMEM((own, width), F32),
            pltpu.VMEM((2, 2 * depth, tokens), BF),
            pltpu.VMEM((2, 2) + box, BF),
            pltpu.VMEM(box, BF),
            pltpu.VMEM(box, BF),
            pltpu.VMEM((6,) + box, BF),
            *[pltpu.VMEM(size, BF) for size in sizes],
            like(mixed), like(q_rot), like(k_rot), like(v_low), like(q_hat), like(k_hat), like(inv),
            like(cosine), like(sine), like(probs),
            pltpu.VMEM((tokens, cols), BF),
            pltpu.VMEM((tokens, 3 * cols), BF),
            pltpu.VMEM((8, 8, tokens), F32),
            pltpu.VMEM((4, 2 * width // gains.shape[1], gains.shape[1]), F32),
            pltpu.VMEM((count,) + gains.shape, F32),
            DMA((64 + 3 * len(kinds),)), DMA((3,)), DMA((number,)),
            DMA((number,)), DMA((number,)),
            DMA((number,)), DMA((number,)),
            DMA((7,)), DMA((7,)),
            DMA((7,)), DMA((7,)),
            DMA((9,)), DMA((9,)),
            DMA((7,)), DMA((7,)),
            DMA((3,)), DMA((3,)),
            DMA((count - 1,)), DMA((count - 1,)),
            DMA((6,)),
        ],
        compiler_params=pltpu.CompilerParams(
            collective_id=1, has_side_effects=True, vmem_limit_bytes=63 * MIB
        ),
        name="backward",
    )(
        gffn, hidden, gate, up, mid, rows, full, mixed, q_rot, k_rot, v_low, q_hat, k_hat, inv, cosine, sine, probs,
        normed, ainv, top, gains, part_gain,
    )


def local(
    inputs,
    seg_ids,
    positions,
    w_query,
    w_key,
    w_value,
    w_out,
    query_gain,
    key_gain,
    attn_gain,
    w_gate,
    w_up,
    w_down,
    ffn_gain,
    out_grad,
    count,
    tensor,
):
    index = lax.axis_index("fsdp")
    own_rows, width = inputs.shape
    group_rows = seg_ids.shape[0]
    depth = width // count

    heads_here, part = query_gain.shape
    heads_half = heads_here // 2
    cols = heads_half * HD
    sizes = heads_here * part

    def placed(values, copies):
        size = values.shape[-1]
        here = jnp.arange(size * count, dtype=jnp.int32) // size == index
        return jnp.where(here, jnp.tile(values, copies), 0).reshape(-1, heads_here * HD)

    packed = jnp.concatenate(
        [
            placed(attn_gain, count),
            placed(ffn_gain, count),
            placed(jnp.concatenate([query_gain, key_gain]), (1, count)),
        ]
    )
    packed = jnp.pad(packed, ((0, -packed.shape[0] % 16), (0, 0)))

    token_rows = jnp.pad(jnp.stack([positions, seg_ids]).astype(F32), ((0, 6), (0, 0)))
    freq = np.float32(ROPE_THETA) ** (-(np.arange(HD // 2, dtype=np.float32) * 2) / np.float32(HD))
    angles = np.zeros((8, HD), np.float32)
    angles[0] = np.concatenate([freq, freq])
    angles[1] = np.concatenate([-np.ones(HD // 2), np.ones(HD // 2)])
    turned = depth % 128 != 0

    (
        full, gains, query_rot, key_rot, value_low, query_hat, key_hat, invs, attn_normed, attn_inv, gate_raw, up_raw,
        output, partial_ffn_gain, probs, cosine, sine, rows_grad_ffn, mixed_low, hidden_low, all_rows, rows_mid,
    ) = run_forward(
        count, inputs, w_query, w_key, w_value, w_out.T if turned else w_out, w_gate, w_up,
        w_down.T if turned else w_down, packed, token_rows, angles, out_grad,
    )
    wide = width // gains.shape[1]
    (
        grad_rows, gain_sums, _, _, _, _, zbuf_r, zbuf_c,
    ) = run_backward(
        count, rows_grad_ffn, hidden_low, gate_raw, up_raw, rows_mid, all_rows, full, mixed_low, query_rot,
        key_rot, value_low, query_hat, key_hat, invs, cosine, sine, probs, attn_normed, attn_inv,
        out_grad, gains, partial_ffn_gain,
    )

    (
        sum_query, sum_key, sum_value, sum_out, sum_gate, sum_up, sum_down, grad_inputs, output,
    ) = run_settle(count, cols, hidden_low.shape[0], zbuf_r, zbuf_c, grad_rows, output)

    def own_gain(row):
        return lax.dynamic_slice_in_dim(gain_sums[row * wide : (row + 1) * wide].reshape(-1), index * depth, depth)

    def own_head_gain(row):
        values = gain_sums[2 * wide + row].reshape(heads_here, HD)
        return lax.dynamic_slice_in_dim(values, index * part, part, 1)

    return (
        output,
        grad_inputs,
        sum_query,
        sum_key,
        sum_value,
        sum_out[:, :depth],
        own_head_gain(0),
        own_head_gain(1),
        own_gain(0),
        sum_gate,
        sum_up,
        sum_down[:, :depth],
        own_gain(1),
    )


def solution(mesh):
    count = mesh.shape["fsdp"]
    tensor = mesh.shape["tensor"]
    tokens = P(("fsdp", "tensor"), None)
    rows = P("fsdp", "tensor")
    columns = P("tensor", "fsdp")
    line = P("fsdp")

    def body(*arrays):
        return local(*arrays, count=count, tensor=tensor)

    return jax.shard_map(
        body,
        mesh=mesh,
        in_specs=(
            tokens, line, line, rows, rows, rows, columns, columns, columns, line,
            rows, rows, columns, line, tokens,
        ),
        out_specs=(
            tokens, tokens, rows, rows, rows, columns, columns, columns, line,
            rows, rows, columns, line,
        ),
        check_vma=False,
    )
```

time: 1860 us -> 531 us (0.29)
  waiting for transfers between devices: 1520 us -> 0 us
  Pallas kernels: 0 us -> 515 us
  matrix products: 139 us -> 0 us
  blocking collectives: 90.8 us -> 0 us
  other arithmetic: 45.7 us -> 2.08 us
  local copies, waits for them, and re-layouts: 32.5 us -> 4.64 us
    reduce_scatter x11 -> x0, waiting for transfers between devices: 851 us -> none  [the longest x1 151 us: local(): lax.psum_scatter(wgrad_down.astype(jnp.bfloat16), 'fsdp', scatter_dimensi...]
    all_gather x11 -> x0, waiting for transfers between devices: 572 us -> none  [the longest x1 122 us: local(): lax.all_gather(w_gate, 'fsdp', axis=0, tiled=True)]
    pallas_call x0 -> x3, Pallas kernels: none -> 515 us  [the longest x1 282 us: run_forward(): pl.pallas_call(functools.partial(forward_kernel, count), out_shape=outs,...]
    dot_general x27 -> x0, matrix products: 139 us -> none  [the longest x7 42.4 us: contract_first(): lax.dot_general(left, right, (((0,), (0,)), ((), ())), preferred_element_...]
    unnamed x28 -> x0, waiting for transfers between devices: 100 us -> none
    all_gather x4 -> x0, blocking collectives: 74.8 us -> none  [the longest x1 22.5 us: local(): lax.all_gather(query_gain, 'fsdp', axis=1, tiled=True)]
    unnamed x99 -> x13, local copies, waits for them, and re-layouts: 24.9 us -> 1.35 us
    convert_element_type x17 -> x1, other arithmetic: 22.1 us -> 0.71 us  [local(): jnp.stack([positions, seg_ids]).astype(F32)]
  transfers between devices with their start and end apart: 25 -> 0, of which waited for: 23 -> 0; matrix products, arithmetic and copies ran while one was open for 7% -> 0% of each run, Pallas kernels for 0% -> 0%
where the time goes in v1:
time: 531 us; the launch traced here: 523 us
  Pallas kernels  515 us (97%)
    pallas_call x1, Pallas kernels, run_forward(): pl.pallas_call(functools.partial(forward_kernel, count), out_shape=outs,...  282 us
    pallas_call x1, Pallas kernels, run_backward(): pl.pallas_call(functools.partial(backward_kernel, count, pieces), out_sha...  225 us

profile of v1, /device:TPU:0, one launch (start us, length us, event | category | flops | bytes accessed | tf_op | source)
XLA Modules:
  0.0 522.8 jit_solution(11528279443136019309)
XLA Ops:
  0.6 0.0 copy-start
  0.7 0.6 copy-done
  1.3 0.7 broadcast_bitcast_fusion.1
  2.0 0.7 pad_maximum_fusion
  2.8 0.1 tile.38
  2.9 0.6 fusion.4.gains_ref
  3.5 0.7 add_convert_fusion
  4.2 0.6 pad.9.tokens_ref
  4.8 282.1 %forward.1 = (bf16[16,2048,256]{2,1,0:T(8,128)(2,1)}, f32[16,512]{1,0:T(8,128)}, bf16[1024,256]{1,0:T(8,128)(2,1)}, bf16[1024,256]{1,0:T(8,128)(2,1)}, bf16[1024...) custom-call(bf16[128,2048]{1,0:T(8,128)(2,1)} %rows_ref.1, ...), custom_call_target="tpu_custom_call" | custom-call | tf_op jit(solution)/shard_map/forward/pallas_call | solution.py:729
  286.9 224.8 %backward.1 = (f32[128,2048]{1,0:T(8,128)}, f32[16,512]{1,0:T(8,128)}, bf16[16,2,256,1024]{3,2,1,0:T(8,128)(2,1)}, bf16[8,2,256,1024]{3,2,1,0:T(8,128)(2,1)}, bf...) custom-call(bf16[8,128,2048]{2,1,0:T(8,128)(2,1)} %get-tuple-element, ...), custom_call_target="tpu_custom_call" | custom-call | tf_op jit(solution)/shard_map/backward/pallas_call | solution.py:1390
  511.8 0.0 copy-start.1
  511.8 0.0 copy-start.2
  511.8 8.2 %settle.1 = (f32[256,512]{1,0:T(8,128)}, f32[256,512]{1,0:T(8,128)}, f32[256,512]{1,0:T(8,128)}, f32[512,256]{1,0:T(8,128)}, f32[256,2048]{1,0:T(8,128)}, /*inde...) custom-call(bf16[16,256,1024]{2,1,0:T(8,128)(2,1)} %get-tuple-element.69.zbuf_r, ...), custom_call_target="tpu_custom_call" | custom-call | tf_op jit(solution)/shard_map/settle/pallas_call | solution.py:1349
  520.0 0.0 copy-done.2
  520.1 0.6 dynamic_slice.14
  520.7 0.6 dynamic_slice.15
  521.4 0.7 constant_dynamic-slice_fusion
  522.0 0.6 constant_dynamic-slice_fusion.1
  522.7 0.0 copy-done.1
  (12 shorter events, 0.1 us)
Async XLA Ops:
  0.6 0.7 copy-start
  511.8 10.9 %copy-start.1 = (bf16[256]{0:T(256)(128)(2,1)S(1)}, bf16[256]{0:T(256)(128)(2,1)}, u32[]{:S(2)}) copy-start(bf16[256]{0:T(256)(128)(2,1)} %param.25) | copy-start | bytes 1540
  511.8 8.2 %copy-start.2 = (f32[16,512]{1,0:T(8,128)S(1)}, f32[16,512]{1,0:T(8,128)}, u32[]{:S(2)}) copy-start(f32[16,512]{1,0:T(8,128)} %get-tuple-element.79) | copy-start | bytes 98308

commit v2 on v1

--- a/solution.py
+++ b/solution.py
@@ -228,9 +228,9 @@
         first = pair * 4 + core * 2
         m = pl.ds(pl.multiple_of(first * own, 2 * own), 2 * own)
 
-        @pl.loop(0, width // 256)
+        @pl.loop(0, width // 512)
         def _(n):
-            at = pl.ds(pl.multiple_of(n * 256, 256), 256)
+            at = pl.ds(pl.multiple_of(n * 512, 512), 512)
             out = product_last(left_ref[m, :], right[at, lanes]).astype(BF)
             parts[first, :, at] = out[:own]
             parts[first + 1, :, at] = out[own:]
@@ -845,15 +845,15 @@
         self.launch()
         ring = self.ring.at[p % 2]
         wide = self.pieces[p][2]
-        step = 256
+        step = 512 if wide % 512 == 0 else 256
 
         @pl.loop(0, wide // step)
         def _(n):
             lanes = pl.ds(pl.multiple_of(first + n * step, step), step)
             to = pl.ds(pl.multiple_of(n * step, step), step)
-            for low in (0, 1):
-                rows = left[low * self.depth : (low + 1) * self.depth]
-                ring[low, : self.depth, to] = product(rows, right[:, lanes]).astype(BF)
+            out = product(left[...], right[:, lanes]).astype(BF)
+            ring[0, : self.depth, to] = out[: self.depth]
+            ring[1, : self.depth, to] = out[self.depth :]
 
         self.local[p].start()
         self.made = p + 1
@@ -867,12 +867,14 @@
         pitch = wide // number
         tokens = right.shape[0] * right.shape[1]
         cols = right[:, :, self.owner(p)].reshape(tokens, 2 * self.depth)
-        for c in range(number):
-            out = product(left[c * rows : (c + 1) * rows], cols).astype(BF)
-            for low in (0, 1):
-                ring[low, :rows, c * pitch : c * pitch + self.depth] = out[
-                    :, low * self.depth : (low + 1) * self.depth
-                ]
+        together = 2 if number % 2 == 0 else 1
+        for c in range(0, number, together):
+            out = product(left[c * rows : (c + together) * rows], cols).astype(BF)
+            for r in range(together):
+                for low in (0, 1):
+                    ring[low, :rows, (c + r) * pitch : (c + r) * pitch + self.depth] = out[
+                        r * rows : (r + 1) * rows, low * self.depth : (low + 1) * self.depth
+                    ]
         self.local[p].start()
         self.made = p + 1
 
@@ -1034,10 +1036,10 @@
             once(*firsts[j])
             at = 2 * (j % 2)
 
-            @pl.loop(0, 4)
+            @pl.loop(0, 2)
             def _(i):
-                m = pl.ds(pl.multiple_of(i * 2 * own, 2 * own), 2 * own)
-                left = rows_a[pl.ds(i * 2, 2)].reshape(2 * own, width)
+                m = pl.ds(pl.multiple_of(i * big, big), big)
+                left = rows_a[pl.ds(i * 4, 4)].reshape(big, width)
                 grad = product(left, weights[:, j * cols : (j + 1) * cols])
                 acts[m, 2 * j * cols : (2 * j + 1) * cols] = (grad * floats[at, m]).astype(BF)
                 acts[m, (2 * j + 1) * cols : (2 * j + 2) * cols] = (grad * floats[at + 1, m]).astype(BF)
@@ -1097,10 +1099,10 @@
     def out_back():
         once(*late["att"], *late["rest"])
 
-        @pl.loop(0, 4)
+        @pl.loop(0, 2)
         def _(i):
-            m = pl.ds(pl.multiple_of(i * 2 * own, 2 * own), 2 * own)
-            left = rows_c[pl.ds(i * 2, 2)].reshape(2 * own, width)
+            m = pl.ds(pl.multiple_of(i * big, big), big)
+            left = rows_c[pl.ds(i * 4, 4)].reshape(big, width)
             datt[m] = product(left, weights[:, 3 * cols : 4 * cols]).astype(BF)
 
     scale = HD ** (-0.5)

time: 531 us -> 526 us (level)
  Pallas kernels: 515 us -> 507 us
    pallas_call x1, Pallas kernels: 225 us -> 214 us  [run_backward(): pl.pallas_call(functools.partial(backward_kernel, count, pieces), out_sha...]
where the time goes in v2:
time: 526 us; the launch traced here: 515 us
  Pallas kernels  507 us (96%)
    pallas_call x1, Pallas kernels, run_forward(): pl.pallas_call(functools.partial(forward_kernel, count), out_shape=outs,...  285 us
    pallas_call x1, Pallas kernels, run_backward(): pl.pallas_call(functools.partial(backward_kernel, count, pieces), out_sha...  214 us

profile of v2, /device:TPU:0, one launch (start us, length us, event | category | flops | bytes accessed | tf_op | source)
XLA Modules:
  0.0 515.3 jit_solution(2216150177815467464)
XLA Ops:
  0.6 0.0 copy-start
  0.7 0.6 copy-done
  1.3 0.7 broadcast_bitcast_fusion.1
  2.0 0.7 pad_maximum_fusion
  2.8 0.1 tile.38
  2.9 0.6 fusion.4.gains_ref
  3.5 0.7 add_convert_fusion
  4.2 0.6 pad.9.tokens_ref
  4.8 284.7 %forward.1 = (bf16[16,2048,256]{2,1,0:T(8,128)(2,1)}, f32[16,512]{1,0:T(8,128)}, bf16[1024,256]{1,0:T(8,128)(2,1)}, bf16[1024,256]{1,0:T(8,128)(2,1)}, bf16[1024...) custom-call(bf16[128,2048]{1,0:T(8,128)(2,1)} %rows_ref.1, ...), custom_call_target="tpu_custom_call" | custom-call | tf_op jit(solution)/shard_map/forward/pallas_call | solution.py:729
  289.5 214.5 %backward.1 = (f32[128,2048]{1,0:T(8,128)}, f32[16,512]{1,0:T(8,128)}, bf16[16,2,256,1024]{3,2,1,0:T(8,128)(2,1)}, bf16[8,2,256,1024]{3,2,1,0:T(8,128)(2,1)}, bf...) custom-call(bf16[8,128,2048]{2,1,0:T(8,128)(2,1)} %get-tuple-element, ...), custom_call_target="tpu_custom_call" | custom-call | tf_op jit(solution)/shard_map/backward/pallas_call | solution.py:1392
  504.0 0.0 copy-start.1
  504.0 0.0 copy-start.2
  504.0 8.2 %settle.1 = (f32[256,512]{1,0:T(8,128)}, f32[256,512]{1,0:T(8,128)}, f32[256,512]{1,0:T(8,128)}, f32[512,256]{1,0:T(8,128)}, f32[256,2048]{1,0:T(8,128)}, /*inde...) custom-call(bf16[16,256,1024]{2,1,0:T(8,128)(2,1)} %get-tuple-element.69.zbuf_r, ...), custom_call_target="tpu_custom_call" | custom-call | tf_op jit(solution)/shard_map/settle/pallas_call | solution.py:1351
  512.2 0.0 copy-done.2
  512.3 0.6 dynamic_slice.14
  512.9 0.6 dynamic_slice.15
  513.6 0.7 constant_dynamic-slice_fusion
  514.2 0.6 constant_dynamic-slice_fusion.1
  514.9 0.0 copy-done.1
  (12 shorter events, 0.1 us)
Async XLA Ops:
  0.6 0.7 copy-start
  504.0 10.9 %copy-start.1 = (bf16[256]{0:T(256)(128)(2,1)S(1)}, bf16[256]{0:T(256)(128)(2,1)}, u32[]{:S(2)}) copy-start(bf16[256]{0:T(256)(128)(2,1)} %param.25) | copy-start | bytes 1540
  504.0 8.2 %copy-start.2 = (f32[16,512]{1,0:T(8,128)S(1)}, f32[16,512]{1,0:T(8,128)}, u32[]{:S(2)}) copy-start(f32[16,512]{1,0:T(8,128)} %get-tuple-element.79) | copy-start | bytes 98308

commit v3 on v2

--- a/solution.py
+++ b/solution.py
@@ -240,9 +240,13 @@
 
 def exchange_sums(place, stats, columns, sends, recvs):
     tokens = stats.shape[2]
+    rows = [jnp.transpose(jnp.broadcast_to(column, (tokens, 128)))[0:1] for column in columns]
+    stats[place.slot()] = jnp.concatenate(rows + [jnp.zeros((6, tokens), F32)], axis=0)
+    return exchange_rows(place, stats, sends, recvs)
+
+
+def exchange_rows(place, stats, sends, recvs):
     mine = place.slot()
-    rows = [jnp.transpose(jnp.broadcast_to(column, (tokens, 128)))[0:1] for column in columns]
-    stats[mine] = jnp.concatenate(rows + [jnp.zeros((6, tokens), F32)], axis=0)
     copies = []
     for i, (p, c, s) in enumerate(place.group()):
         copy = send(stats.at[mine], stats.at[mine], sends, recvs, i, place.peer(p, c, s))
@@ -935,7 +939,7 @@
     gbuf_r, gbuf_c, ybuf_r, ybuf_c, zbuf_r, zbuf_c,
     rows_a, rows_c, hidden, acts, floats, weights, parts, from_core, from_chips, total, resid, turned, ring,
     came, have, ready, kept0, kept1, kept2, kept3, kept4, kept5,
-    mixed, q_rot, k_rot, v_low, q_hat, k_hat, inv, cos_ref, sin_ref, probs_ref, datt, dqkv, stats, side_sums, all_sums,
+    mixed, q_rot, k_rot, v_low, q_hat, k_hat, inv, cos_ref, sin_ref, probs_ref, datt, dqkv, stats, part_sums, inner_sums, side_sums, all_sums,
     big_loads, loads, local, ysends, yrecvs, zsends, zrecvs, rsends, rrecvs, r2sends, r2recvs, gsends, grecvs,
     ssends, srecvs, xsends, xrecvs, fsends, frecvs, keeps,
 ):
@@ -1143,26 +1147,35 @@
     def rotate_back():
         gain_at = pl.ds(pl.multiple_of(place.pair * cols, cols), cols)
         norm_gains = [gains_ref[2 * wide + which : 2 * wide + which + 1, gain_at] for which in (0, 1)]
-        gain_parts, inners = [], []
-        for which, hat in ((0, q_hat), (1, k_hat)):
-            pieces_of = []
-            for h in range(heads):
-                lanes = slice(h * HD, (h + 1) * HD)
-                value = floats[which, :, lanes]
-                value = value * cos_ref[...] - pltpu.roll(value, HD // 2, 1) * sin_ref[...]
-                weighted = value * hat[:, lanes]
-                gain_parts.append(jnp.sum(weighted, axis=0, keepdims=True))
-                part = norm_gains[which][:, lanes]
-                pieces_of.append(jnp.sum(weighted * part, axis=1, keepdims=True))
-                floats[which, :, lanes] = value * part
-            inners.append(sum(pieces_of[1:], pieces_of[0]))
-        inner_copies.extend(exchange_sums(place, stats, inners, ssends, srecvs))
+        mine = place.slot()
+        stats[mine] = jnp.zeros(stats.shape[1:], F32)
+        part_sums[...] = jnp.zeros(part_sums.shape, F32)
+
+        @pl.loop(0, 8)
+        def _(i):
+            m = pl.ds(pl.multiple_of(i * own, own), own)
+            cosine = cos_ref[m]
+            sine = sin_ref[m]
+            for which, hat in ((0, q_hat), (1, k_hat)):
+                inner = 0.0
+                for h in range(heads):
+                    lanes = slice(h * HD, (h + 1) * HD)
+                    value = floats[which, m, lanes]
+                    value = value * cosine - pltpu.roll(value, HD // 2, 1) * sine
+                    weighted = value * hat[m, lanes]
+                    part_sums[which, :, lanes] += jnp.sum(weighted.reshape(own // 8, 8, HD), axis=0)
+                    part = norm_gains[which][:, lanes]
+                    inner = inner + jnp.sum(weighted * part, axis=1, keepdims=True)
+                    floats[which, m, lanes] = value * part
+                stats[mine, which : which + 1, m] = jnp.transpose(jnp.broadcast_to(inner, (own, 128)))[0:1]
+
+        inner_copies.extend(exchange_rows(place, stats, ssends, srecvs))
         for copy in side_copies:
             copy.wait_recv()
         side = side_sums[0]
         for t in range(1, side_sums.shape[0]):
             side = side + side_sums[t]
-        gain_rows = [jnp.concatenate(gain_parts[w * heads : (w + 1) * heads], axis=1) for w in (0, 1)]
+        gain_rows = [jnp.sum(part_sums[w], axis=0, keepdims=True) for w in (0, 1)]
         upper = place.pair == 1
         gain_rows = [
             jnp.concatenate([jnp.where(upper, 0.0, row), jnp.where(upper, row, 0.0)], axis=1) for row in gain_rows
@@ -1178,13 +1191,17 @@
             all_copies.append(copy)
 
     def query_key():
-        sums = finish_sums(stats, inner_copies) / width
-        for which, hat in ((0, q_hat), (1, k_hat)):
-            lanes_inner = over_lanes(sums[which : which + 1])
-            for h in range(heads):
-                lanes = slice(h * HD, (h + 1) * HD)
-                value = inv[which] * (floats[which, :, lanes] - hat[:, lanes] * lanes_inner)
-                dqkv[:, which * cols + h * HD : which * cols + (h + 1) * HD] = value.astype(BF)
+        inner_sums[...] = finish_sums(stats, inner_copies) / width
+
+        @pl.loop(0, 8)
+        def _(i):
+            m = pl.ds(pl.multiple_of(i * own, own), own)
+            for which, hat in ((0, q_hat), (1, k_hat)):
+                inner = over_lanes(inner_sums[which : which + 1, m])
+                for h in range(heads):
+                    lanes = slice(h * HD, (h + 1) * HD)
+                    value = inv[which, m] * (floats[which, m, lanes] - hat[m, lanes] * inner)
+                    dqkv[m, which * cols + h * HD : which * cols + (h + 1) * HD] = value.astype(BF)
 
     def first_again(pair):
         if pair:
@@ -1415,6 +1432,8 @@
             pltpu.VMEM((tokens, cols), BF),
             pltpu.VMEM((tokens, 3 * cols), BF),
             pltpu.VMEM((8, 8, tokens), F32),
+            pltpu.VMEM((2, 8, cols), F32),
+            pltpu.VMEM((8, tokens), F32),
             pltpu.VMEM((4, 2 * width // gains.shape[1], gains.shape[1]), F32),
             pltpu.VMEM((count,) + gains.shape, F32),
             DMA((64 + 3 * len(kinds),)), DMA((3,)), DMA((number,)),

time: 526 us -> 526 us (level)
  no operation moved by 1% of the time
where the time goes in v3:
time: 526 us; the launch traced here: 516 us
  Pallas kernels  508 us (97%)
    pallas_call x1, Pallas kernels, run_forward(): pl.pallas_call(functools.partial(forward_kernel, count), out_shape=outs,...  285 us
    pallas_call x1, Pallas kernels, run_backward(): pl.pallas_call(functools.partial(backward_kernel, count, pieces), out_sha...  215 us

profile of v3, /device:TPU:0, one launch (start us, length us, event | category | flops | bytes accessed | tf_op | source)
XLA Modules:
  0.0 515.7 jit_solution(17222593580483467058)
XLA Ops:
  0.6 0.0 copy-start
  0.7 0.6 copy-done
  1.3 0.7 broadcast_bitcast_fusion.1
  2.0 0.7 pad_maximum_fusion
  2.8 0.1 tile.38
  2.9 0.6 fusion.4.gains_ref
  3.5 0.7 add_convert_fusion
  4.2 0.6 pad.9.tokens_ref
  4.8 284.7 %forward.1 = (bf16[16,2048,256]{2,1,0:T(8,128)(2,1)}, f32[16,512]{1,0:T(8,128)}, bf16[1024,256]{1,0:T(8,128)(2,1)}, bf16[1024,256]{1,0:T(8,128)(2,1)}, bf16[1024...) custom-call(bf16[128,2048]{1,0:T(8,128)(2,1)} %rows_ref.1, ...), custom_call_target="tpu_custom_call" | custom-call | tf_op jit(solution)/shard_map/forward/pallas_call | solution.py:733
  289.5 214.9 %backward.1 = (f32[128,2048]{1,0:T(8,128)}, f32[16,512]{1,0:T(8,128)}, bf16[16,2,256,1024]{3,2,1,0:T(8,128)(2,1)}, bf16[8,2,256,1024]{3,2,1,0:T(8,128)(2,1)}, bf...) custom-call(bf16[8,128,2048]{2,1,0:T(8,128)(2,1)} %get-tuple-element, ...), custom_call_target="tpu_custom_call" | custom-call | tf_op jit(solution)/shard_map/backward/pallas_call | solution.py:1409
  504.4 0.0 copy-start.1
  504.4 0.0 copy-start.2
  504.4 8.2 %settle.1 = (f32[256,512]{1,0:T(8,128)}, f32[256,512]{1,0:T(8,128)}, f32[256,512]{1,0:T(8,128)}, f32[512,256]{1,0:T(8,128)}, f32[256,2048]{1,0:T(8,128)}, /*inde...) custom-call(bf16[16,256,1024]{2,1,0:T(8,128)(2,1)} %get-tuple-element.69.zbuf_r, ...), custom_call_target="tpu_custom_call" | custom-call | tf_op jit(solution)/shard_map/settle/pallas_call | solution.py:1368
  512.7 0.0 copy-done.2
  512.7 0.6 dynamic_slice.14
  513.3 0.6 dynamic_slice.15
  514.0 0.7 constant_dynamic-slice_fusion
  514.6 0.6 constant_dynamic-slice_fusion.1
  515.3 0.0 copy-done.1
  (12 shorter events, 0.1 us)
Async XLA Ops:
  0.6 0.7 copy-start
  504.4 10.9 %copy-start.1 = (bf16[256]{0:T(256)(128)(2,1)S(1)}, bf16[256]{0:T(256)(128)(2,1)}, u32[]{:S(2)}) copy-start(bf16[256]{0:T(256)(128)(2,1)} %param.25) | copy-start | bytes 1540
  504.4 8.2 %copy-start.2 = (f32[16,512]{1,0:T(8,128)S(1)}, f32[16,512]{1,0:T(8,128)}, u32[]{:S(2)}) copy-start(f32[16,512]{1,0:T(8,128)} %get-tuple-element.79) | copy-start | bytes 98308
